TPU v7x, 768 devices: a whole 4x8x12 slice. The times are simulated.
768 devices in a mesh: ta: 32 (over z_lo, y), sa: 24 (over z_hi, x, core).
Axes of the slice: x: 4, y: 8, z: 12 (z_hi: 3, z_lo: 4; z = z_hi * 4 + z_lo), core: 2. Of those that a mesh axis runs over, the one named last changes fastest.
Arguments:
- source_field: bfloat16 [2, 3, 4, 32, 32, 24, 128], P(None, None, None, None, 'ta', 'sa'), may hold values from -6 to 6
- gauge_links: bfloat16 [2, 4, 3, 3, 32, 24, 128], P(None, None, None, None, 'ta', 'sa'), may hold values from -6 to 6
- clover: bfloat16 [2, 2, 3, 3, 32, 24, 128], P(None, None, None, None, 'ta', 'sa'), may hold values from -4 to 4
- eigenvectors: bfloat16 [2, 3, 64, 32, 24, 128], P(None, None, None, 'ta', 'sa'), may hold values from -0.046875 to 0.046875
Outputs:
- result_field: bfloat16 [2, 3, 4, 32, 32, 24, 128], P(None, None, None, None, 'ta', 'sa')
- perambulator: float32 [2, 32, 64, 128], P(None, 'ta')
All inputs are finite; a program needn't handle non-finite values.
Results may differ from a plain program's by a relative error of at most 0.0045.
Values may be sent and summed in bfloat16 or wider, within the bound.
No kernel may reach another device: no remote copies, remote signals or barrier semaphores. Data moves between devices by JAX's collectives and lax.ppermute only.
A program may use at most 32 MiB of HBM per device.

v0:
```python
import jax
import jax.numpy as jnp
from jax import lax
from jax.sharding import PartitionSpec as P

LY = 16
LX = 8


SPIN_REAL = [[[0, 0], [0, 0]], [[0, -1], [1, 0]], [[0, 0], [0, 0]], [[1, 0], [0, 1]]]
SPIN_IMAG = [[[0, -1], [-1, 0]], [[0, 0], [0, 0]], [[-1, 0], [0, 1]], [[0, 0], [0, 0]]]
KAPPA = 0.125


def passed_along(shard, axis, by):
    length = lax.axis_size(axis)
    return lax.ppermute(shard, axis, [(i, (i + by) % length) for i in range(length)])


def spin_apply(field, direction, dagger):
    real_tab = SPIN_REAL[direction]
    imag_tab = SPIN_IMAG[direction]
    rows = []
    for s in range(2):
        sum_real = 0.0
        sum_imag = 0.0
        for t in range(2):
            if dagger:
                factor_re = real_tab[t][s]
                factor_im = -imag_tab[t][s]
            else:
                factor_re = real_tab[s][t]
                factor_im = imag_tab[s][t]
            part_re = field[0, :, t]
            part_im = field[1, :, t]
            if factor_re != 0:
                sum_real = sum_real + factor_re * part_re
                sum_imag = sum_imag + factor_re * part_im
            if factor_im != 0:
                sum_real = sum_real - factor_im * part_im
                sum_imag = sum_imag + factor_im * part_re
        rows.append(jnp.stack([sum_real, sum_imag]))
    return jnp.stack(rows, axis=2)


def half_minus(field, direction):
    spins = field.astype(jnp.float32)
    return (spins[:, :, 0:2] - spin_apply(spins[:, :, 2:4], direction, False)).astype(jnp.bfloat16)


def half_plus(field, direction):
    spins = field.astype(jnp.float32)
    return spins[:, :, 0:2] + spin_apply(spins[:, :, 2:4], direction, False)


def rebuild_minus(part, direction):
    return jnp.concatenate([part, -spin_apply(part, direction, True)], axis=2)


def rebuild_plus(part, direction):
    return jnp.concatenate([part, spin_apply(part, direction, True)], axis=2)


def color_apply(links, part, dagger):
    link_re = links[0].astype(jnp.float32)
    link_im = links[1].astype(jnp.float32)
    out_re = 0.0
    out_im = 0.0
    for b in range(3):
        if dagger:
            coef_re = link_re[b]
            coef_im = -link_im[b]
        else:
            coef_re = link_re[:, b]
            coef_im = link_im[:, b]
        coef_re = coef_re[:, None, None]
        coef_im = coef_im[:, None, None]
        part_re = part[0, b][None]
        part_im = part[1, b][None]
        out_re = out_re + coef_re * part_re - coef_im * part_im
        out_im = out_im + coef_re * part_im + coef_im * part_re
    return jnp.stack([out_re, out_im])


def roll_site(field, direction, amount):
    shape = field.shape
    grid = field.reshape(shape[:-1] + (LY, LX))
    axis_pick = -1 if direction == 0 else -2
    return jnp.roll(grid, amount, axis=axis_pick).reshape(shape)


def clover_apply(clover, field):
    spins = field.astype(jnp.float32)
    upper = spins[:, :, 0:2]
    lower = spins[:, :, 2:4]
    upper = upper + color_apply(clover[:, 0], upper, False)
    lower = lower + color_apply(clover[:, 1], lower, False)
    return jnp.concatenate([upper, lower], axis=2)


def shards(source_field, gauge_links, clover, eigenvectors):
    last_slab = lax.axis_index("ta") == lax.axis_size("ta") - 1
    first_slab = lax.axis_index("ta") == 0
    ahead_sign = jnp.where(last_slab, -1.0, 1.0).astype(jnp.float32)
    behind_sign = jnp.where(first_slab, -1.0, 1.0).astype(jnp.float32)
    hopping = jnp.zeros(source_field.shape, jnp.float32)
    for direction in range(4):
        link_now = gauge_links[:, direction]
        minus_part = half_minus(source_field, direction)
        back_part = color_apply(link_now, half_plus(source_field, direction), True).astype(
            jnp.bfloat16
        )
        if direction < 2:
            ahead = roll_site(minus_part, direction, -1).astype(jnp.float32)
            behind = roll_site(back_part, direction, 1).astype(jnp.float32)
        elif direction == 2:
            plane = passed_along(source_field, "sa", -1)
            arrived = half_minus(plane, 2)
            ahead = jnp.concatenate([minus_part[:, :, :, :, :, 1:], arrived], axis=5).astype(
                jnp.float32
            )
            behind_plane = passed_along(back_part, "sa", 1)
            behind = jnp.concatenate([behind_plane, back_part[:, :, :, :, :, :-1]], axis=5).astype(
                jnp.float32
            )
        else:
            plane = passed_along(source_field, "ta", -1)
            arrived = half_minus(plane, 3)
            ahead = jnp.concatenate(
                [
                    minus_part[:, :, :, :, 1:].astype(jnp.float32),
                    arrived.astype(jnp.float32) * ahead_sign,
                ],
                axis=4,
            )
            behind_plane = passed_along(back_part, "ta", 1)
            behind = jnp.concatenate(
                [
                    behind_plane.astype(jnp.float32) * behind_sign,
                    back_part[:, :, :, :, :-1].astype(jnp.float32),
                ],
                axis=4,
            )
        hopping = hopping + rebuild_minus(color_apply(link_now, ahead, False), direction)
        hopping = hopping + rebuild_plus(behind, direction)
    result = (clover_apply(clover, source_field) - KAPPA * hopping).astype(jnp.bfloat16)
    left = eigenvectors.reshape((6, eigenvectors.shape[2]) + eigenvectors.shape[3:])
    flat = result.reshape((6, 4 * result.shape[3]) + result.shape[4:])
    real_part = jnp.einsum("rktzx,rmtzx->tkm", left, flat, preferred_element_type=jnp.float32)
    imag_first = jnp.einsum(
        "rktzx,rmtzx->tkm", left[:3], flat[3:], preferred_element_type=jnp.float32
    )
    imag_second = jnp.einsum(
        "rktzx,rmtzx->tkm", left[3:], flat[:3], preferred_element_type=jnp.float32
    )
    projected = jnp.stack([real_part, imag_first - imag_second])
    perambulator = lax.psum(projected, "sa")
    return (result, perambulator)


def solution(mesh):
    in_specs = (
        P(None, None, None, None, "ta", "sa", None),
        P(None, None, None, None, "ta", "sa", None),
        P(None, None, None, None, "ta", "sa", None),
        P(None, None, None, "ta", "sa", None),
    )
    out_specs = (P(None, None, None, None, "ta", "sa", None), P(None, "ta", None, None))
    return jax.shard_map(shards, mesh=mesh, in_specs=in_specs, out_specs=out_specs, check_vma=False)
```

profile of v0, /device:TPU:1, one launch (start us, length us, event | category | flops | bytes accessed | tf_op | source)
XLA Modules:
  0.0 324.8 jit_solution(2173766975568004259)
XLA Ops:
  7.2 11.4 %collective-permute-start.2 = (bf16[2,3,4,32,1,1,128]{6,3,5,4,2,1,0:T(8,128)(2,1)}, bf16[2,3,4,32,1,1,128]{6,3,5,4,2,1,0:T(8,128)(2,1)}, u32[]{:S(2)}, u32[]{:S(2)}) collective-permute-start(bf16[2,3,4,32,1,1,128]{6,3,5,4,2,1,0:T(8,128)(2,1)} %param.4), channel_id=1, source_target_pairs={{0,744},{24,0},{48,24},{72,48},{96,72},{120,96},{144,120},{168,144... | collective-permute-start | bytes 589832 | tf_op jit(solution)/shard_map/ppermute | solution.py:17
  18.6 3.0 collective-permute-start
  21.6 1.0 convert_element_type.339
  22.7 0.9 copy-done.1
  23.7 0.7 copy-done.20
  24.4 0.6 fusion.64
  25.2 0.6 pad_maximum_fusion.9
  25.9 2.9 collective-permute-start.1
  28.9 0.6 pad_maximum_fusion.10
  29.6 2.7 collective-permute-start.3
  32.3 0.8 slice_bitcast_fusion.76
  33.3 0.7 slice.932
  35.3 0.4 fusion.17
  36.2 0.2 copy.737
  36.4 0.6 slice.966
  38.3 0.4 fusion.19
  38.9 0.8 fusion.68
  39.9 0.9 fusion.13
  40.9 0.6 copy-done.27
  42.0 0.6 slice_bitcast_fusion.33
  42.6 0.6 slice_bitcast_fusion.34
  43.3 0.9 copy-done.4
  44.5 0.6 copy-done.25
  45.7 0.7 copy-done.21
  46.6 0.7 copy-done.23
  47.3 0.6 copy.928
  47.9 0.6 copy.929
  48.5 0.6 copy.930
  49.0 0.6 copy.931
  49.6 0.6 copy.932
  50.2 0.6 copy.933
  51.3 0.8 copy-done.3
  52.5 0.6 copy-done.22
  53.3 0.8 copy-done.6
  54.1 0.8 copy-done.7
  55.0 0.7 copy-done.14
  55.9 0.6 copy-done.9
  56.8 0.9 convert_element_type.369
  57.7 0.9 convert_multiply_fusion
  58.7 1.0 copy_convert_fusion
  60.0 1.0 convert_element_type.372
  61.0 0.9 convert_multiply_fusion.1
  62.0 0.6 copy-done.31
  63.0 1.3 fusion.8
  64.3 0.9 copy-done.5
  65.8 0.7 pad_maximum_fusion.11
  66.5 250.0 %all-reduce.2.cloned.1.call-done = f32[2,1,64,128]{3,2,1,0:T(8,128)} async-done(((f32[2,1,64,128]{3,2,1,0:T(8,128)}), f32[2,1,64,128]{3,2,1,0:T(8,128)}) %all-reduce.2.cloned.1.call-update) | async-done | bytes 65552 | tf_op jit(solution)/shard_map/psum | solution.py:157
  316.5 1.5 copy.971
  (239 shorter events, 8.2 us)
Async XLA Ops:
  7.2 309.3 %all-reduce.2.cloned.1.call-start = ((), (), s32[]{:S(2)}) async-start(), calls=%async_computation | async-start | bytes 131072 | tf_op jit(solution)/shard_map/psum | solution.py:157
  7.2 52.8 %collective-permute-start.2 = (bf16[2,3,4,32,1,1,128]{6,3,5,4,2,1,0:T(8,128)(2,1)}, bf16[2,3,4,32,1,1,128]{6,3,5,4,2,1,0:T(8,128)(2,1)}, u32[]{:S(2)}, u32[]{:S(2)}) collective-permute-start(bf16[2,3,4,32,1,1,128]{6,3,5,4,2,1,0:T(8,128)(2,1)} %param.4), channel_id=1, source_target_pairs={{0,744},{24,0},{48,24},{72,48},{96,72},{120,96},{144,120},{168,144... | collective-permute-start | bytes 589832 | tf_op jit(solution)/shard_map/ppermute | solution.py:17
  18.6 40.1 %collective-permute-start = (bf16[2,3,4,32,1,1,128]{6,3,5,4,2,1,0:T(8,128)(2,1)}, bf16[2,3,4,32,1,1,128]{6,3,5,4,2,1,0:T(8,128)(2,1)}, u32[]{:S(2)}, u32[]{:S(2)}) collective-permute-start(bf16[2,3,4,32,1,1,128]{6,3,5,4,2,1,0:T(8,128)(2,1)} %param.4), channel_id=1, source_target_pairs={{0,23},{1,0},{2,1},{3,2},{4,3},{5,4},{6,5},{7,6},{8,7},{9,8},{10,9... | collective-permute-start | bytes 589832 | tf_op jit(solution)/shard_map/ppermute | solution.py:17
  22.6 0.9 copy-start.1
  23.7 0.7 copy-start.20
  25.9 30.9 %collective-permute-start.1 = (bf16[2,3,2,32,1,1,128]{6,3,1,5,4,2,0:T(8,128)(2,1)}, bf16[2,3,2,32,1,1,128]{6,3,1,5,4,2,0:T(8,128)(2,1)}, u32[]{:S(2)}, u32[]{:S(2)}) collective-permute-start(bf16[2,3,2,32,1,1,128]{6,3,1,5,4,2,0:T(8,128)(2,1)} %pad_maximum_fusion.9), channel_id=1, source_target_pairs={{0,1},{1,2},{2,3},{3,4},{4,5},{5,6},{6,7},{7,8},{8,9},{9,10},{10,1... | collective-permute-start | bytes 294920 | tf_op jit(solution)/shard_map/ppermute | solution.py:17
  29.6 28.1 %collective-permute-start.3 = (bf16[2,3,2,32,1,1,128]{6,3,1,5,4,2,0:T(8,128)(2,1)}, bf16[2,3,2,32,1,1,128]{6,3,1,5,4,2,0:T(8,128)(2,1)}, u32[]{:S(2)}, u32[]{:S(2)}) collective-permute-start(bf16[2,3,2,32,1,1,128]{6,3,1,5,4,2,0:T(8,128)(2,1)} %pad_maximum_fusion.10), channel_id=1, source_target_pairs={{0,24},{24,48},{48,72},{72,96},{96,120},{120,144},{144,168},{168,1... | collective-permute-start | bytes 294920 | tf_op jit(solution)/shard_map/ppermute | solution.py:17
  40.8 0.7 copy-start.27
  40.8 0.7 copy-start.28
  43.3 0.9 copy-start.4
  44.5 0.7 copy-start.25
  44.5 0.7 copy-start.26
  45.7 0.7 copy-start.21
  46.6 0.7 copy-start.23
  46.6 0.7 copy-start.24
  51.1 0.9 copy-start.3
  51.2 1.0 copy-start.2
  52.4 0.7 copy-start.22
  53.3 0.8 copy-start.6
  53.3 0.8 copy-start.8
  54.1 0.8 copy-start.7
  54.9 0.8 copy-start.14
  54.9 0.8 copy-start.15
  54.9 0.8 copy-start.16
  54.9 0.8 copy-start.17
  54.9 0.8 copy-start.18
  55.0 0.8 copy-start.19
  55.8 0.8 copy-start.9
  55.8 0.8 copy-start.10
  55.8 0.8 copy-start.11
  55.8 0.8 copy-start.12
  55.8 0.8 copy-start.13
  62.0 0.7 copy-start.31
  62.0 0.7 copy-start.32
  62.0 0.7 copy-start.33
  62.0 0.7 copy-start.34
  62.0 0.7 copy-start.30
  62.0 0.7 copy-start.29
  64.3 1.3 copy-start
  64.3 1.0 copy-start.5
Sparse Core Ops, SparseCore 0:
  66.6 249.8 all-reduce.1
where the time goes:
time: 330 us; the launch traced here: 325 us
  waiting for transfers between devices  250 us (76%)
  local copies, waits for them, and re-layouts  24.5 us (7%)
  starting transfers between devices  19.9 us (6%)
  between operations  15.4 us (5%)
  other arithmetic  14.5 us (4%)
    psum x1, waiting for transfers between devices, shards(): perambulator = lax.psum(projected, 'sa')  250 us
    ppermute x4, starting transfers between devices, passed_along(): lax.ppermute(shard, axis, [(i, (i + by) % length) for i in range(length)])  19.9 us
    unnamed x127, local copies, waits for them, and re-layouts  17.1 us
  transfers between devices with their start and end apart: 5, of which 1 were waited for; matrix products, arithmetic and copies ran while one was open for 7% of the time, Pallas kernels for 0%

commit v1 on v0

v1 whole, which is shorter than its diff:
```python
import functools

import jax
import jax.numpy as jnp
from jax import lax
from jax.experimental import pallas as pl
from jax.experimental.pallas import tpu as pltpu
from jax.sharding import PartitionSpec as P

KAPPA = 0.125
ROWS = 16
F32 = jnp.float32
BF16 = jnp.bfloat16


def add(a, b):
    return (a[0] + b[0], a[1] + b[1])


def sub(a, b):
    return (a[0] - b[0], a[1] - b[1])


def neg(a):
    return (-a[0], -a[1])


def times_i(a):
    return (-a[1], a[0])


def spin(direction, w):
    if direction == 0:
        return [neg(times_i(w[1])), neg(times_i(w[0]))]
    if direction == 1:
        return [neg(w[1]), w[0]]
    if direction == 2:
        return [neg(times_i(w[0])), times_i(w[1])]
    return [w[0], w[1]]


def spin_dagger(direction, w):
    if direction == 0:
        return [times_i(w[1]), times_i(w[0])]
    if direction == 1:
        return [w[1], neg(w[0])]
    if direction == 2:
        return [times_i(w[0]), neg(times_i(w[1]))]
    return [w[0], w[1]]


def rounded(a):
    return (a[0].astype(BF16).astype(F32), a[1].astype(BF16).astype(F32))


def load_field(ref, rows, spins):
    return [
        [(ref[0, c, s, rows, :].astype(F32), ref[1, c, s, rows, :].astype(F32)) for s in range(spins)]
        for c in range(3)
    ]


def load_matrix(ref, which):
    tiles = [[[ref[q, a, b, :, :].astype(F32) for b in range(3)] for a in range(3)] for q in range(2)]
    return [
        [(tiles[0][a][b][which : which + 1, :], tiles[1][a][b][which : which + 1, :]) for b in range(3)]
        for a in range(3)
    ]


def color_row(matrix, part, a, s, dagger):
    re = im = None
    for b in range(3):
        x_re, x_im = part[b][s]
        if dagger:
            m_re, m_im = matrix[b][a]
            terms = (m_re * x_re + m_im * x_im, m_re * x_im - m_im * x_re)
        else:
            m_re, m_im = matrix[a][b]
            terms = (m_re * x_re - m_im * x_im, m_re * x_im + m_im * x_re)
        re = terms[0] if re is None else re + terms[0]
        im = terms[1] if im is None else im + terms[1]
    return (re, im)


def half(field, direction, plus):
    out = []
    for c in range(3):
        turned = spin(direction, [field[c][2], field[c][3]])
        out.append([(add if plus else sub)(field[c][s], turned[s]) for s in range(2)])
    return out


def store_half(ref, rows, part):
    for c in range(3):
        for s in range(2):
            for q in range(2):
                ref[q, c, s, rows, :] = part[c][s][q].astype(BF16)


def edge_kernel(src, links, hz, gz, ht, gt):
    columns = src.shape[3]
    link = {2: load_matrix(links, 2), 3: load_matrix(links, 3)}
    for at in range(0, columns, ROWS):
        rows = pl.ds(at, ROWS)
        field = load_field(src, rows, 4)
        for direction, h_ref, g_ref in ((2, hz, gz), (3, ht, gt)):
            store_half(h_ref, rows, half(field, direction, False))
            plus = half(field, direction, True)
            back = [[color_row(link[direction], plus, a, s, True) for s in range(2)] for a in range(3)]
            store_half(g_ref, rows, back)


def shift_sites(x, direction, ahead):
    lane = lax.broadcasted_iota(jnp.int32, x.shape, 1)
    if direction == 1:
        return pltpu.roll(x, 120 if ahead else 8, 1)
    if ahead:
        return jnp.where(lane % 8 == 7, pltpu.roll(x, 7, 1), pltpu.roll(x, 127, 1))
    return jnp.where(lane % 8 == 0, pltpu.roll(x, 121, 1), pltpu.roll(x, 1, 1))


def local_kernel(src, links, clover, out):
    columns = src.shape[3]
    link = {0: load_matrix(links, 0), 1: load_matrix(links, 1)}
    clov = [load_matrix(clover, 0), load_matrix(clover, 1)]
    for at in range(0, columns, ROWS):
        rows = pl.ds(at, ROWS)
        field = load_field(src, rows, 4)
        hop = [[None] * 4 for _ in range(3)]
        for direction in range(2):
            minus = half(field, direction, False)
            ahead = [
                [tuple(shift_sites(v, direction, True) for v in rounded(minus[c][s])) for s in range(2)]
                for c in range(3)
            ]
            plus = half(field, direction, True)
            for a in range(3):
                w = [color_row(link[direction], ahead, a, s, False) for s in range(2)]
                g = [
                    tuple(
                        shift_sites(v, direction, False)
                        for v in rounded(color_row(link[direction], plus, a, s, True))
                    )
                    for s in range(2)
                ]
                upper = [add(w[s], g[s]) for s in range(2)]
                lower = spin_dagger(direction, [sub(g[s], w[s]) for s in range(2)])
                for s, v in enumerate(upper + lower):
                    hop[a][s] = v if hop[a][s] is None else add(hop[a][s], v)
        for a in range(3):
            for s in range(4):
                own = add(field[a][s], color_row(clov[s // 2], field, a, s, False))
                for q in range(2):
                    out[q, a, s, rows, :] = own[q] - KAPPA * hop[a][s][q]


def finish_kernel(ta_size, local, links, hz, gz, ht, gt, vectors, result, partial):
    columns = local.shape[3]
    me = lax.axis_index("ta")
    ahead_sign = jnp.where(me == ta_size - 1, -1.0, 1.0).astype(F32)
    behind_sign = jnp.where(me == 0, -1.0, 1.0).astype(F32)
    link_z = load_matrix(links, 2)
    link_t = [[(m[0] * ahead_sign, m[1] * ahead_sign) for m in row] for row in load_matrix(links, 3)]
    for at in range(0, columns, ROWS):
        rows = pl.ds(at, ROWS)
        from_z = load_field(hz, rows, 2)
        from_t = load_field(ht, rows, 2)
        back_z = load_field(gz, rows, 2)
        back_t = load_field(gt, rows, 2)
        for a in range(3):
            wz = [color_row(link_z, from_z, a, s, False) for s in range(2)]
            wt = [color_row(link_t, from_t, a, s, False) for s in range(2)]
            gz_now = back_z[a]
            gt_now = [(v[0] * behind_sign, v[1] * behind_sign) for v in back_t[a]]
            lower_z = spin_dagger(2, [sub(gz_now[s], wz[s]) for s in range(2)])
            for s in range(2):
                upper = add(add(wz[s], gz_now[s]), add(wt[s], gt_now[s]))
                lower = add(lower_z[s], sub(gt_now[s], wt[s]))
                for q in range(2):
                    result[q, a, s, rows, :] = (local[q, a, s, rows, :] - KAPPA * upper[q]).astype(BF16)
                    result[q, a, s + 2, rows, :] = (local[q, a, s + 2, rows, :] - KAPPA * lower[q]).astype(BF16)
    total = None
    contract = (((1,), (1,)), ((), ()))
    for c in range(3):
        left_re = vectors[0, c]
        left_im = vectors[1, c]
        for q in range(2):
            right = result[q, c].reshape(4 * columns, result.shape[4])
            left = [left_re, -left_im] if q == 0 else [left_im, left_re]
            term = lax.dot_general(jnp.concatenate(left, axis=0), right, contract, preferred_element_type=F32)
            total = term if total is None else total + term
    partial[...] = total.astype(BF16).reshape(partial.shape)


def call(body, outs, operands, flops):
    vmem = pl.BlockSpec(memory_space=pltpu.VMEM)
    moved = sum(x.size * x.dtype.itemsize for x in list(outs) + list(operands))
    return pl.pallas_call(
        body,
        out_shape=outs,
        in_specs=[vmem] * len(operands),
        out_specs=[vmem] * len(outs),
        compiler_params=pltpu.CompilerParams(vmem_limit_bytes=32 * 2**20),
        cost_estimate=pl.CostEstimate(flops=flops, bytes_accessed=moved, transcendentals=0),
    )(*operands)


def gathered_sum(x, groups):
    both = lax.all_gather(x, "sa", axis_index_groups=groups).astype(F32)
    return lax.reduce_precision(both[0] + both[1], 8, 7).astype(BF16)


def sum_over_blocks(partial, size):
    plane = 8
    planes = size // plane
    cores = [[i, i + 1] for i in range(0, size, 2)]
    starts = range(0, size, plane)
    even = [[z + 4 * p + c, z + 4 * p + 2 + c] for z in starts for p in range(2) for c in range(2)]
    odd = [[z + 2 + c, z + 4 + c] for z in starts for c in range(2)]
    odd += [[z + c, z + 6 + c] for z in starts for c in range(2)]
    s = gathered_sum(partial, cores)
    s = gathered_sum(s, even)
    s = gathered_sum(s, odd)
    pairs = []
    for i in range(size):
        z, r = divmod(i, plane)
        step = 1 if i % 2 else planes - 1
        pairs.append((i, ((z + step) % planes) * plane + r))
    other = lax.all_gather(lax.ppermute(s, "sa", pairs), "sa", axis_index_groups=cores)
    z = lax.axis_index("sa") // plane
    own, nxt, last = s.astype(F32), other[0].astype(F32), other[1].astype(F32)
    first = jnp.where(z == 0, own, jnp.where(z == 1, last, nxt))
    second = jnp.where(z == 0, nxt, jnp.where(z == 1, own, last))
    third = jnp.where(z == 0, last, jnp.where(z == 1, nxt, own))
    return first + second + third


def shards(source_field, gauge_links, clover, eigenvectors):
    sites = source_field.shape[-1]
    columns = source_field.shape[3]
    ta, sa = lax.axis_size("ta"), lax.axis_size("sa")
    src = source_field.reshape(2, 3, 4, columns, sites)
    links = gauge_links.reshape(2, 4, 3, 3, sites).transpose(0, 2, 3, 1, 4)
    clov = clover.reshape(2, 2, 3, 3, sites).transpose(0, 2, 3, 1, 4)
    vectors = eigenvectors.reshape(2, 3, eigenvectors.shape[2], sites)
    half_shape = jax.ShapeDtypeStruct((2, 3, 2, columns, sites), BF16)
    points = columns * sites

    hz, gz, ht, gt = call(edge_kernel, [half_shape] * 4, (src, links), 500 * points)

    def passed(x, axis, size, by):
        return lax.ppermute(x, axis, [(i, (i + by) % size) for i in range(size)])

    hz_in = passed(hz, "sa", sa, -1)
    gz_in = passed(gz, "sa", sa, 1)
    ht_in = passed(ht, "ta", ta, -1)
    gt_in = passed(gt, "ta", ta, 1)
    (local,) = call(
        local_kernel,
        [jax.ShapeDtypeStruct((2, 3, 4, columns, sites), F32)],
        (src, links, clov),
        2000 * points,
    )
    result, partial = call(
        functools.partial(finish_kernel, ta),
        [
            jax.ShapeDtypeStruct((2, 3, 4, columns, sites), BF16),
            jax.ShapeDtypeStruct((2, vectors.shape[2], 4 * columns), BF16),
        ],
        (local, links, hz_in, gz_in, ht_in, gt_in, vectors),
        1000 * points,
    )
    perambulator = sum_over_blocks(partial, sa)
    return result.reshape(source_field.shape), perambulator[:, None]


def solution(mesh):
    in_specs = (
        P(None, None, None, None, "ta", "sa", None),
        P(None, None, None, None, "ta", "sa", None),
        P(None, None, None, None, "ta", "sa", None),
        P(None, None, None, "ta", "sa", None),
    )
    out_specs = (P(None, None, None, None, "ta", "sa", None), P(None, "ta", None, None))
    return jax.shard_map(shards, mesh=mesh, in_specs=in_specs, out_specs=out_specs, check_vma=False)
```

time: 330 us -> 66.3 us (0.20); the launches traced: 325 us -> 65.9 us
  waiting for transfers between devices: 250 us -> 10.9 us
  blocking collectives: 0 us -> 25.8 us
  local copies, waits for them, and re-layouts: 24.5 us -> 1.65 us
  between operations: 15.4 us -> 0.79 us
  other arithmetic: 14.5 us -> 0.73 us
  starting transfers between devices: 19.9 us -> 24.2 us
    psum x1 -> x0, waiting for transfers between devices: 250 us -> none  [shards(): perambulator = lax.psum(projected, 'sa')]
    all_gather x0 -> x4, blocking collectives: none -> 25.8 us  [the longest x3 20.6 us: gathered_sum(): both = lax.all_gather(x, 'sa', axis_index_groups=groups).astype(F32)]
    unnamed x127 -> x8, local copies, waits for them, and re-layouts: 17.1 us -> 1.65 us
    ppermute x4 -> x5, waiting for transfers between devices: 0.01 us -> 10.9 us  [the longest x4 6.77 us: passed(): return lax.ppermute(x, axis, [(i, (i + by) % size) for i in range(size)])]
    convert_element_type x10 -> x6, other arithmetic: 6.85 us -> 0.06 us  [the longest x3 0.03 us: gathered_sum(): return lax.reduce_precision(both[0] + both[1], 8, 7).astype(BF16)]
    another operation x27 -> x0, other arithmetic: 4.39 us -> none  [the longest x9 2.31 us: color_apply(): return jnp.stack([out_re, out_im])]
    ppermute x4 -> x5, starting transfers between devices: 19.9 us -> 24.2 us  [the longest x4 19.6 us: passed(): return lax.ppermute(x, axis, [(i, (i + by) % size) for i in range(size)])]
    slice x28 -> x0, local copies, waits for them, and re-layouts: 3.59 us -> none  [the longest x4 1.44 us: roll_site(): return jnp.roll(grid, amount, axis=axis_pick).reshape(shape)]
  transfers between devices with their start and end apart: 5 -> 5, of which waited for: 1 -> 3; matrix products, arithmetic and copies ran while one was open for 7% -> 0% of each run, Pallas kernels for 0% -> 1%
where the time goes in v1:
time: 66.3 us; the launch traced here: 65.9 us
  blocking collectives  25.8 us (39%)
  starting transfers between devices  24.2 us (37%)
  waiting for transfers between devices  10.9 us (16%)
  Pallas kernels  1.91 us (3%)
  local copies, waits for them, and re-layouts  1.65 us (2%)
  between operations  0.79 us (1%)
  other arithmetic  0.73 us (1%)
    all_gather x3, blocking collectives, gathered_sum(): both = lax.all_gather(x, 'sa', axis_index_groups=groups).astype(F32)  20.6 us
    ppermute x4, starting transfers between devices, passed(): return lax.ppermute(x, axis, [(i, (i + by) % size) for i in range(size)])  19.6 us
    ppermute x4, waiting for transfers between devices, passed(): return lax.ppermute(x, axis, [(i, (i + by) % size) for i in range(size)])  6.77 us
    all_gather x1, blocking collectives, sum_over_blocks(): lax.all_gather(lax.ppermute(s, 'sa', pairs), 'sa', axis_index_groups=cores)  5.18 us
    ppermute x1, starting transfers between devices, sum_over_blocks(): lax.ppermute(s, 'sa', pairs)  4.53 us
    ppermute x1, waiting for transfers between devices, sum_over_blocks(): lax.ppermute(s, 'sa', pairs)  4.11 us
    pallas_call x3, Pallas kernels, call(): pl.pallas_call(body, out_shape=outs, in_specs=[vmem] * len(operands), out...  1.91 us
    unnamed x8, local copies, waits for them, and re-layouts  1.65 us
  transfers between devices with their start and end apart: 5, of which 3 were waited for; matrix products, arithmetic and copies ran while one was open for 0% of the time, Pallas kernels for 1%

profile of v1, /device:TPU:1, one launch (start us, length us, event | category | flops | bytes accessed | tf_op | source)
XLA Modules:
  0.0 65.9 jit_solution(14479021613924855466)
XLA Ops:
  0.6 0.0 copy-start
  0.6 0.9 %copy-done = bf16[2,3,4,32,1,1,128]{6,3,5,4,2,1,0:T(8,128)(2,1)S(1)} copy-done((bf16[2,3,4,32,1,1,128]{6,3,5,4,2,1,0:T(8,128)(2,1)S(1)}, bf16[2,3,4,32,1,1,128]{6,3,5,4,2,1,0:T(8,128)(2,1)}, u32[]{:S(2)}) %copy-start) | copy-done | bytes 196632
  1.6 0.0 copy-start.1
  1.6 0.7 %copy-done.1 = bf16[2,4,3,3,1,1,128]{6,1,5,4,3,2,0:T(4,128)(2,1)S(1)} copy-done((bf16[2,4,3,3,1,1,128]{6,1,5,4,3,2,0:T(4,128)(2,1)S(1)}, bf16[2,4,3,3,1,1,128]{6,1,5,4,3,2,0:T(4,128)(2,1)}, u32[]{:S(2)}) %copy-start.1) | copy-done | bytes 18456
  2.3 0.2 shard_map.60
  2.5 0.0 copy-start.3
  2.5 12.4 %collective-permute-start = (bf16[2,3,2,32,128]{4,3,2,1,0:T(8,128)(2,1)S(1)}, bf16[2,3,2,32,128]{4,3,2,1,0:T(8,128)(2,1)S(1)}, u32[]{:S(2)}, u32[]{:S(2)}) collective-permute-start(bf16[2,3,2,32,128]{4,3,2,1,0:T(8,128)(2,1)S(1)} %get-tuple-element.8), channel_id=1, source_target_pairs={{0,23},{1,0},{2,1},{3,2},{4,3},{5,4},{6,5},{7,6},{8,7},{9,8},{10,9... | collective-permute-start | bytes 294920 | tf_op jit(solution)/shard_map/ppermute | solution.py:253
  14.9 1.9 %collective-permute-start.1 = (bf16[2,3,2,32,128]{4,3,2,1,0:T(8,128)(2,1)S(1)}, bf16[2,3,2,32,128]{4,3,2,1,0:T(8,128)(2,1)S(1)}, u32[]{:S(2)}, u32[]{:S(2)}) collective-permute-start(bf16[2,3,2,32,128]{4,3,2,1,0:T(8,128)(2,1)S(1)} %get-tuple-element.9), channel_id=1, source_target_pairs={{0,1},{1,2},{2,3},{3,4},{4,5},{5,6},{6,7},{7,8},{8,9},{9,10},{10,1... | collective-permute-start | bytes 294920 | tf_op jit(solution)/shard_map/ppermute | solution.py:253
  16.9 2.6 %collective-permute-start.2 = (bf16[2,3,2,32,128]{4,3,2,1,0:T(8,128)(2,1)S(1)}, bf16[2,3,2,32,128]{4,3,2,1,0:T(8,128)(2,1)S(1)}, u32[]{:S(2)}, u32[]{:S(2)}) collective-permute-start(bf16[2,3,2,32,128]{4,3,2,1,0:T(8,128)(2,1)S(1)} %get-tuple-element.10), channel_id=1, source_target_pairs={{0,744},{24,0},{48,24},{72,48},{96,72},{120,96},{144,120},{168,144... | collective-permute-start | bytes 294920 | tf_op jit(solution)/shard_map/ppermute | solution.py:253
  19.5 2.7 %collective-permute-start.3 = (bf16[2,3,2,32,128]{4,3,2,1,0:T(8,128)(2,1)S(1)}, bf16[2,3,2,32,128]{4,3,2,1,0:T(8,128)(2,1)S(1)}, u32[]{:S(2)}, u32[]{:S(2)}) collective-permute-start(bf16[2,3,2,32,128]{4,3,2,1,0:T(8,128)(2,1)S(1)} %get-tuple-element.11), channel_id=1, source_target_pairs={{0,24},{24,48},{48,72},{72,96},{96,120},{120,144},{144,168},{168,1... | collective-permute-start | bytes 294920 | tf_op jit(solution)/shard_map/ppermute | solution.py:253
  22.2 0.0 copy-done.3
  22.2 0.0 copy-start.2
  22.2 0.6 shard_map.59.local
  22.8 0.0 collective-permute-done.hz
  22.9 0.1 collective-permute-done.1.gz
  22.9 0.0 collective-permute-done.2.ht
  22.9 6.7 %collective-permute-done.3.gt = bf16[2,3,2,32,128]{4,3,2,1,0:T(8,128)(2,1)S(1)} collective-permute-done((bf16[2,3,2,32,128]{4,3,2,1,0:T(8,128)(2,1)S(1)}, bf16[2,3,2,32,128]{4,3,2,1,0:T(8,128)(2,1)S(1)}, u32[]{:S(2)}, u32[]{:S(2)}) %collective-permute-start.3) | collective-permute-done | bytes 98336 | tf_op jit(solution)/shard_map/ppermute | solution.py:253
  29.6 0.0 copy-done.2
  29.6 1.0 %shard_map.61 = (bf16[2,3,4,32,128]{4,3,2,1,0:T(8,128)(2,1)}, bf16[2,64,128]{2,1,0:T(8,128)(2,1)S(1)}) custom-call(f32[2,3,4,32,128]{4,3,2,1,0:T(8,128)S(1)} %shard_map.59.local, bf16[2,3,3,4,128]{4,3,2,1,0:T(4,128)(2,1)S(1)} %bitcast.34, bf16[2,3,2,32,128]{4,3,2,1,0:T(8,128)(2,1)S(1)} %collective-permute-done.hz, ...), custom_call_target="tpu_custom_call" | custom-call | flops 4096000 | bytes 1132544 | tf_op jit(solution)/shard_map/pallas_call | solution.py:199
  30.7 12.5 %all-gather = bf16[4,64,128]{2,1,0:T(8,128)(2,1)S(1)} all-gather(bf16[2,64,128]{2,1,0:T(8,128)(2,1)S(1)} %get-tuple-element.13), channel_id=2, replica_groups={{0,1},{2,3},{4,5},{6,7},{8,9},{10,11},{12,13},{14,15},{16,17},{18,19},{..., dimensions={0}, use_global_device_ids=true | all-gather | bytes 98304 | tf_op jit(solution)/shard_map/all_gather | solution.py:210
  43.2 3.4 %all_gather.22 = bf16[2,2,64,128]{3,2,1,0:T(8,128)(2,1)S(1)} all-gather(bf16[1,2,64,128]{3,2,1,0:T(8,128)(2,1)S(1)} %fusion.9), channel_id=1, replica_groups={{0,2},{1,3},{4,6},{5,7},{8,10},{9,11},{12,14},{13,15},{16,18},{17,19},{..., dimensions={0}, use_global_device_ids=true | all-gather | bytes 98304 | tf_op jit(solution)/shard_map/all_gather | solution.py:210
  46.7 4.7 %all_gather.23 = bf16[2,2,64,128]{3,2,1,0:T(8,128)(2,1)S(1)} all-gather(bf16[1,2,64,128]{3,2,1,0:T(8,128)(2,1)S(1)} %fusion.6), channel_id=1, replica_groups={{2,4},{3,5},{10,12},{11,13},{18,20},{19,21},{0,6},{1,7},{8,14},{9,15},{..., dimensions={0}, use_global_device_ids=true | all-gather | bytes 98304 | tf_op jit(solution)/shard_map/all_gather | solution.py:210
  51.4 4.5 %collective-permute-start.4 = (bf16[2,64,128]{2,1,0:T(8,128)(2,1)S(1)}, bf16[2,64,128]{2,1,0:T(8,128)(2,1)S(1)}, u32[]{:S(2)}, u32[]{:S(2)}) collective-permute-start(bf16[2,64,128]{2,1,0:T(8,128)(2,1)S(1)} %fusion.10), channel_id=1, source_target_pairs={{0,16},{1,9},{2,18},{3,11},{4,20},{5,13},{6,22},{7,15},{8,0},{9,17... | collective-permute-start | bytes 98312 | tf_op jit(solution)/shard_map/ppermute | solution.py:230
  56.0 4.1 %collective-permute-done.4 = bf16[2,64,128]{2,1,0:T(8,128)(2,1)S(1)} collective-permute-done((bf16[2,64,128]{2,1,0:T(8,128)(2,1)S(1)}, bf16[2,64,128]{2,1,0:T(8,128)(2,1)S(1)}, u32[]{:S(2)}, u32[]{:S(2)}) %collective-permute-start.4) | collective-permute-done | bytes 32800 | tf_op jit(solution)/shard_map/ppermute | solution.py:230
  60.1 5.2 %all-gather.1 = bf16[4,64,128]{2,1,0:T(8,128)(2,1)S(1)} all-gather(bf16[2,64,128]{2,1,0:T(8,128)(2,1)S(1)} %collective-permute-done.4), channel_id=3, replica_groups={{0,1},{2,3},{4,5},{6,7},{8,9},{10,11},{12,13},{14,15},{16,17},{18,19},{..., dimensions={0}, use_global_device_ids=true | all-gather | bytes 98304 | tf_op jit(solution)/shard_map/all_gather | solution.py:230
  65.3 0.7 %fusion.2 = f32[2,1,64,128]{3,2,1,0:T(8,128)} fusion(bf16[4,64,128]{2,1,0:T(8,128)(2,1)S(1)} %all-gather.1, pred[]{:T(512)S(6)} %eq.5, pred[]{:T(512)S(6)} %eq.4, f32[2,2,64,128]{3,2,1,0:T(8,128)S(1)} %convert_element_type.74), kind=kLoop, calls=%fused_computation.8 | loop fusion | flops 229376 | bytes 262146
  (6 shorter events, 0.1 us)
Async XLA Ops:
  0.6 0.9 %copy-start = (bf16[2,3,4,32,1,1,128]{6,3,5,4,2,1,0:T(8,128)(2,1)S(1)}, bf16[2,3,4,32,1,1,128]{6,3,5,4,2,1,0:T(8,128)(2,1)}, u32[]{:S(2)}) copy-start(bf16[2,3,4,32,1,1,128]{6,3,5,4,2,1,0:T(8,128)(2,1)} %param.4) | copy-start | bytes 589828
  1.6 0.7 %copy-start.1 = (bf16[2,4,3,3,1,1,128]{6,1,5,4,3,2,0:T(4,128)(2,1)S(1)}, bf16[2,4,3,3,1,1,128]{6,1,5,4,3,2,0:T(4,128)(2,1)}, u32[]{:S(2)}) copy-start(bf16[2,4,3,3,1,1,128]{6,1,5,4,3,2,0:T(4,128)(2,1)} %param.5) | copy-start | bytes 55300
  2.5 19.7 %copy-start.3 = (bf16[2,2,3,3,1,1,128]{6,1,5,4,3,2,0:T(2,128)(2,1)S(1)}, bf16[2,2,3,3,1,1,128]{6,1,5,4,3,2,0:T(2,128)(2,1)}, u32[]{:S(2)}) copy-start(bf16[2,2,3,3,1,1,128]{6,1,5,4,3,2,0:T(2,128)(2,1)} %param.6) | copy-start | bytes 27652
  2.5 20.3 %collective-permute-start = (bf16[2,3,2,32,128]{4,3,2,1,0:T(8,128)(2,1)S(1)}, bf16[2,3,2,32,128]{4,3,2,1,0:T(8,128)(2,1)S(1)}, u32[]{:S(2)}, u32[]{:S(2)}) collective-permute-start(bf16[2,3,2,32,128]{4,3,2,1,0:T(8,128)(2,1)S(1)} %get-tuple-element.8), channel_id=1, source_target_pairs={{0,23},{1,0},{2,1},{3,2},{4,3},{5,4},{6,5},{7,6},{8,7},{9,8},{10,9... | collective-permute-start | bytes 294920 | tf_op jit(solution)/shard_map/ppermute | solution.py:253
  14.9 8.0 %collective-permute-start.1 = (bf16[2,3,2,32,128]{4,3,2,1,0:T(8,128)(2,1)S(1)}, bf16[2,3,2,32,128]{4,3,2,1,0:T(8,128)(2,1)S(1)}, u32[]{:S(2)}, u32[]{:S(2)}) collective-permute-start(bf16[2,3,2,32,128]{4,3,2,1,0:T(8,128)(2,1)S(1)} %get-tuple-element.9), channel_id=1, source_target_pairs={{0,1},{1,2},{2,3},{3,4},{4,5},{5,6},{6,7},{7,8},{8,9},{9,10},{10,1... | collective-permute-start | bytes 294920 | tf_op jit(solution)/shard_map/ppermute | solution.py:253
  16.9 6.0 %collective-permute-start.2 = (bf16[2,3,2,32,128]{4,3,2,1,0:T(8,128)(2,1)S(1)}, bf16[2,3,2,32,128]{4,3,2,1,0:T(8,128)(2,1)S(1)}, u32[]{:S(2)}, u32[]{:S(2)}) collective-permute-start(bf16[2,3,2,32,128]{4,3,2,1,0:T(8,128)(2,1)S(1)} %get-tuple-element.10), channel_id=1, source_target_pairs={{0,744},{24,0},{48,24},{72,48},{96,72},{120,96},{144,120},{168,144... | collective-permute-start | bytes 294920 | tf_op jit(solution)/shard_map/ppermute | solution.py:253
  19.5 10.1 %collective-permute-start.3 = (bf16[2,3,2,32,128]{4,3,2,1,0:T(8,128)(2,1)S(1)}, bf16[2,3,2,32,128]{4,3,2,1,0:T(8,128)(2,1)S(1)}, u32[]{:S(2)}, u32[]{:S(2)}) collective-permute-start(bf16[2,3,2,32,128]{4,3,2,1,0:T(8,128)(2,1)S(1)} %get-tuple-element.11), channel_id=1, source_target_pairs={{0,24},{24,48},{48,72},{72,96},{96,120},{120,144},{144,168},{168,1... | collective-permute-start | bytes 294920 | tf_op jit(solution)/shard_map/ppermute | solution.py:253
  22.2 7.5 %copy-start.2 = (bf16[2,3,64,1,1,128]{5,2,4,3,1,0:T(8,128)(2,1)S(1)}, bf16[2,3,64,1,1,128]{5,2,4,3,1,0:T(8,128)(2,1)}, u32[]{:S(2)}) copy-start(bf16[2,3,64,1,1,128]{5,2,4,3,1,0:T(8,128)(2,1)} %param.7) | copy-start | bytes 294916
  51.4 8.7 %collective-permute-start.4 = (bf16[2,64,128]{2,1,0:T(8,128)(2,1)S(1)}, bf16[2,64,128]{2,1,0:T(8,128)(2,1)S(1)}, u32[]{:S(2)}, u32[]{:S(2)}) collective-permute-start(bf16[2,64,128]{2,1,0:T(8,128)(2,1)S(1)} %fusion.10), channel_id=1, source_target_pairs={{0,16},{1,9},{2,18},{3,11},{4,20},{5,13},{6,22},{7,15},{8,0},{9,17... | collective-permute-start | bytes 98312 | tf_op jit(solution)/shard_map/ppermute | solution.py:230

commit v2 on v1

--- a/solution.py
+++ b/solution.py
@@ -91,24 +91,38 @@
     return out
 
 
-def store_half(ref, rows, part):
-    for c in range(3):
-        for s in range(2):
-            for q in range(2):
-                ref[q, c, s, rows, :] = part[c][s][q].astype(BF16)
-
-
-def edge_kernel(src, links, hz, gz, ht, gt):
+def edge_kernel(ta_size, src_hbm, links_hbm, to_core, to_first, to_second, to_third, src, links, sems):
+    copies = [
+        pltpu.make_async_copy(src_hbm, src, sems.at[0]),
+        pltpu.make_async_copy(links_hbm, links, sems.at[1]),
+    ]
+    for copy in copies:
+        copy.start()
+    for copy in copies:
+        copy.wait()
     columns = src.shape[3]
-    link = {2: load_matrix(links, 2), 3: load_matrix(links, 3)}
+    link_z, link_t = load_matrix(links, 2), load_matrix(links, 3)
+    me = lax.axis_index("ta")
+    even_z = lax.axis_index("sa") % 2 == 0
+    even_t = me % 2 == 0
+    last = me >= ta_size - 2
     for at in range(0, columns, ROWS):
         rows = pl.ds(at, ROWS)
         field = load_field(src, rows, 4)
-        for direction, h_ref, g_ref in ((2, hz, gz), (3, ht, gt)):
-            store_half(h_ref, rows, half(field, direction, False))
-            plus = half(field, direction, True)
-            back = [[color_row(link[direction], plus, a, s, True) for s in range(2)] for a in range(3)]
-            store_half(g_ref, rows, back)
+        minus_z, minus_t = half(field, 2, False), half(field, 3, False)
+        plus_z, plus_t = half(field, 2, True), half(field, 3, True)
+        for a in range(3):
+            for s in range(2):
+                back_z = color_row(link_z, plus_z, a, s, True)
+                back_t = color_row(link_t, plus_t, a, s, True)
+                for q in range(2):
+                    to_core[q, a, s, rows, :] = jnp.where(even_z, back_z[q], minus_z[a][s][q]).astype(BF16)
+                    chip = jnp.where(even_z, minus_z[a][s][q], back_z[q])
+                    even = jnp.where(even_t, back_t[q], minus_t[a][s][q])
+                    odd = jnp.where(even_t, minus_t[a][s][q], back_t[q])
+                    to_first[q, a, s, rows, :] = jnp.where(last, even, chip).astype(BF16)
+                    to_second[q, a, s, rows, :] = odd.astype(BF16)
+                    to_third[q, a, s, rows, :] = jnp.where(last, chip, even).astype(BF16)
 
 
 def shift_sites(x, direction, ahead):
@@ -155,19 +169,28 @@
                     out[q, a, s, rows, :] = own[q] - KAPPA * hop[a][s][q]
 
 
-def finish_kernel(ta_size, local, links, hz, gz, ht, gt, vectors, result, partial):
+def chosen(first, a, b):
+    return [[tuple(jnp.where(first, p, q) for p, q in zip(v, w)) for v, w in zip(x, y)] for x, y in zip(a, b)]
+
+
+def finish_kernel(ta_size, local, links, cores, first, second, third, vectors, result, partial):
     columns = local.shape[3]
     me = lax.axis_index("ta")
+    core = lax.axis_index("sa") % 2
+    even_z = core == 0
+    even_t = me % 2 == 0
+    last = me >= ta_size - 2
     ahead_sign = jnp.where(me == ta_size - 1, -1.0, 1.0).astype(F32)
     behind_sign = jnp.where(me == 0, -1.0, 1.0).astype(F32)
     link_z = load_matrix(links, 2)
     link_t = [[(m[0] * ahead_sign, m[1] * ahead_sign) for m in row] for row in load_matrix(links, 3)]
     for at in range(0, columns, ROWS):
         rows = pl.ds(at, ROWS)
-        from_z = load_field(hz, rows, 2)
-        from_t = load_field(ht, rows, 2)
-        back_z = load_field(gz, rows, 2)
-        back_t = load_field(gt, rows, 2)
+        one, three = load_field(first, rows, 2), load_field(third, rows, 2)
+        near, far = load_field(cores.at[1 - core], rows, 2), chosen(last, three, one)
+        from_z, back_z = chosen(even_z, near, far), chosen(even_z, far, near)
+        near, far = chosen(last, one, three), load_field(second, rows, 2)
+        from_t, back_t = chosen(even_t, near, far), chosen(even_t, far, near)
         for a in range(3):
             wz = [color_row(link_z, from_z, a, s, False) for s in range(2)]
             wt = [color_row(link_t, from_t, a, s, False) for s in range(2)]
@@ -190,17 +213,18 @@
             left = [left_re, -left_im] if q == 0 else [left_im, left_re]
             term = lax.dot_general(jnp.concatenate(left, axis=0), right, contract, preferred_element_type=F32)
             total = term if total is None else total + term
-    partial[...] = total.astype(BF16).reshape(partial.shape)
-
-
-def call(body, outs, operands, flops):
+    partial[...] = total.reshape(partial.shape)
+
+
+def call(body, outs, operands, flops, in_specs=None, scratch_shapes=()):
     vmem = pl.BlockSpec(memory_space=pltpu.VMEM)
     moved = sum(x.size * x.dtype.itemsize for x in list(outs) + list(operands))
     return pl.pallas_call(
         body,
         out_shape=outs,
-        in_specs=[vmem] * len(operands),
+        in_specs=in_specs or [vmem] * len(operands),
         out_specs=[vmem] * len(outs),
+        scratch_shapes=scratch_shapes,
         compiler_params=pltpu.CompilerParams(vmem_limit_bytes=32 * 2**20),
         cost_estimate=pl.CostEstimate(flops=flops, bytes_accessed=moved, transcendentals=0),
     )(*operands)
@@ -220,8 +244,9 @@
     odd = [[z + 2 + c, z + 4 + c] for z in starts for c in range(2)]
     odd += [[z + c, z + 6 + c] for z in starts for c in range(2)]
     s = gathered_sum(partial, cores)
-    s = gathered_sum(s, even)
-    s = gathered_sum(s, odd)
+    row = [[z + 2 * x + c for x in range(4)] for z in starts for c in range(2)]
+    four = lax.all_to_all(jnp.broadcast_to(s[None], (4,) + s.shape), "sa", 0, 0, axis_index_groups=row).astype(F32)
+    s = lax.reduce_precision((four[0] + four[1]) + (four[2] + four[3]), 8, 7).astype(BF16)
     pairs = []
     for i in range(size):
         z, r = divmod(i, plane)
@@ -247,15 +272,33 @@
     half_shape = jax.ShapeDtypeStruct((2, 3, 2, columns, sites), BF16)
     points = columns * sites
 
-    hz, gz, ht, gt = call(edge_kernel, [half_shape] * 4, (src, links), 500 * points)
-
-    def passed(x, axis, size, by):
-        return lax.ppermute(x, axis, [(i, (i + by) % size) for i in range(size)])
-
-    hz_in = passed(hz, "sa", sa, -1)
-    gz_in = passed(gz, "sa", sa, 1)
-    ht_in = passed(ht, "ta", ta, -1)
-    gt_in = passed(gt, "ta", ta, 1)
+    to_core, to_first, to_second, to_third = call(
+        functools.partial(edge_kernel, ta),
+        [half_shape] * 4,
+        (src, links),
+        500 * points,
+        in_specs=[pl.BlockSpec(memory_space=pl.ANY)] * 2,
+        scratch_shapes=[
+            pltpu.VMEM(src.shape, BF16),
+            pltpu.VMEM(links.shape, BF16),
+            pltpu.SemaphoreType.DMA((2,)),
+        ],
+    )
+
+    def place(t, z):
+        return (t % ta) * sa + z % sa
+
+    def along_z(slabs):
+        return [(place(t, z), place(t, z + (1 if z % 2 else -1))) for t in slabs for z in range(sa)]
+
+    def along_t(slabs, parity):
+        return [(place(t, z), place(t + (1 if t % 2 == parity else -1), z)) for t in slabs for z in range(sa)]
+
+    most, rest = range(ta - 2), range(ta - 2, ta)
+    first = lax.ppermute(to_first, ("ta", "sa"), along_z(most) + along_t(rest, 0))
+    second = lax.ppermute(to_second, ("ta", "sa"), along_t(range(ta), 1))
+    third = lax.ppermute(to_third, ("ta", "sa"), along_t(most, 0) + along_z(rest))
+    cores = lax.all_gather(to_core, "sa", axis_index_groups=[[i, i + 1] for i in range(0, sa, 2)])
     (local,) = call(
         local_kernel,
         [jax.ShapeDtypeStruct((2, 3, 4, columns, sites), F32)],
@@ -266,9 +309,9 @@
         functools.partial(finish_kernel, ta),
         [
             jax.ShapeDtypeStruct((2, 3, 4, columns, sites), BF16),
-            jax.ShapeDtypeStruct((2, vectors.shape[2], 4 * columns), BF16),
+            jax.ShapeDtypeStruct((2, vectors.shape[2], 4 * columns), F32),
         ],
-        (local, links, hz_in, gz_in, ht_in, gt_in, vectors),
+        (local, links, cores, first, second, third, vectors),
         1000 * points,
     )
     perambulator = sum_over_blocks(partial, sa)

time: 66.3 us -> 55.9 us (0.84)
  the two profiles are of different devices: /device:TPU:1 before, /device:TPU:241 now
where the time goes in v2:
time: 55.9 us; the launch traced here: 55.5 us
  blocking collectives  32.7 us (58%)
  starting transfers between devices  12.6 us (23%)
  waiting for transfers between devices  4.83 us (9%)
  Pallas kernels  2.29 us (4%)
  local copies, waits for them, and re-layouts  1.68 us (3%)
  between operations  0.79 us (1%)
  other arithmetic  0.71 us (1%)
    all_gather x1, blocking collectives, shards(): lax.all_gather(to_core, 'sa', axis_index_groups=[[i, i + 1] for i in rang...  12.2 us
    all_gather x1, blocking collectives, gathered_sum(): both = lax.all_gather(x, 'sa', axis_index_groups=groups).astype(F32)  9.12 us
    all_to_all x1, blocking collectives, sum_over_blocks(): lax.all_to_all(jnp.broadcast_to(s[None], (4,) + s.shape), 'sa', 0, 0, axi...  7.23 us
    ppermute x1, waiting for transfers between devices, sum_over_blocks(): lax.ppermute(s, 'sa', pairs)  4.82 us
    ppermute x1, starting transfers between devices, shards(): second = lax.ppermute(to_second, ('ta', 'sa'), along_t(range(ta), 1))  4.35 us
    all_gather x1, blocking collectives, sum_over_blocks(): lax.all_gather(lax.ppermute(s, 'sa', pairs), 'sa', axis_index_groups=cores)  4.13 us
    ppermute x1, starting transfers between devices, sum_over_blocks(): lax.ppermute(s, 'sa', pairs)  3.71 us
    ppermute x1, starting transfers between devices, shards(): lax.ppermute(to_first, ('ta', 'sa'), along_z(most) + along_t(rest, 0))  2.31 us
  transfers between devices with their start and end apart: 4, of which 1 were waited for; matrix products, arithmetic and copies ran while one was open for 0% of the time, Pallas kernels for 1%

profile of v2, /device:TPU:241, one launch (start us, length us, event | category | flops | bytes accessed | tf_op | source)
XLA Modules:
  0.0 55.5 jit_solution(18341931564727392340)
XLA Ops:
  0.6 0.0 copy-start
  0.6 0.9 %copy-done = bf16[2,3,4,32,1,1,128]{6,3,5,4,2,1,0:T(8,128)(2,1)S(1)} copy-done((bf16[2,3,4,32,1,1,128]{6,3,5,4,2,1,0:T(8,128)(2,1)S(1)}, bf16[2,3,4,32,1,1,128]{6,3,5,4,2,1,0:T(8,128)(2,1)}, u32[]{:S(2)}) %copy-start) | copy-done | bytes 196632
  1.6 0.0 copy-start.1
  1.6 0.7 %copy-done.1 = bf16[2,4,3,3,1,1,128]{6,1,5,4,3,2,0:T(4,128)(2,1)S(1)} copy-done((bf16[2,4,3,3,1,1,128]{6,1,5,4,3,2,0:T(4,128)(2,1)S(1)}, bf16[2,4,3,3,1,1,128]{6,1,5,4,3,2,0:T(4,128)(2,1)}, u32[]{:S(2)}) %copy-start.1) | copy-done | bytes 18456
  2.3 0.0 copy-start.4
  2.3 0.5 shard_map.60
  2.8 2.3 %collective-permute-start = (bf16[2,3,2,32,128]{4,3,2,1,0:T(8,128)(2,1)S(1)}, bf16[2,3,2,32,128]{4,3,2,1,0:T(8,128)(2,1)S(1)}, u32[]{:S(2)}, u32[]{:S(2)}) collective-permute-start(bf16[2,3,2,32,128]{4,3,2,1,0:T(8,128)(2,1)S(1)} %get-tuple-element.9), channel_id=1, source_target_pairs={{0,23},{1,2},{2,1},{3,4},{4,3},{5,6},{6,5},{7,8},{8,7},{9,10},{10,... | collective-permute-start | bytes 294920 | tf_op jit(solution)/shard_map/ppermute | solution.py:298
  5.1 4.4 %collective-permute-start.1 = (bf16[2,3,2,32,128]{4,3,2,1,0:T(8,128)(2,1)S(1)}, bf16[2,3,2,32,128]{4,3,2,1,0:T(8,128)(2,1)S(1)}, u32[]{:S(2)}, u32[]{:S(2)}) collective-permute-start(bf16[2,3,2,32,128]{4,3,2,1,0:T(8,128)(2,1)S(1)} %get-tuple-element.10), channel_id=1, source_target_pairs={{0,744},{1,745},{2,746},{3,747},{4,748},{5,749},{6,750},{7,751},{8... | collective-permute-start | bytes 294920 | tf_op jit(solution)/shard_map/ppermute | solution.py:299
  9.5 2.2 %collective-permute-start.2 = (bf16[2,3,2,32,128]{4,3,2,1,0:T(8,128)(2,1)S(1)}, bf16[2,3,2,32,128]{4,3,2,1,0:T(8,128)(2,1)S(1)}, u32[]{:S(2)}, u32[]{:S(2)}) collective-permute-start(bf16[2,3,2,32,128]{4,3,2,1,0:T(8,128)(2,1)S(1)} %get-tuple-element.11), channel_id=1, source_target_pairs={{0,24},{1,25},{2,26},{3,27},{4,28},{5,29},{6,30},{7,31},{8,32},{9,... | collective-permute-start | bytes 294920 | tf_op jit(solution)/shard_map/ppermute | solution.py:300
  11.7 0.0 copy-done.4
  11.7 0.6 %shard_map.59.local = f32[2,3,4,32,128]{4,3,2,1,0:T(8,128)S(1)} custom-call(bf16[2,3,4,32,128]{4,3,2,1,0:T(8,128)(2,1)S(1)} %bitcast.30, bf16[2,3,3,4,128]{4,3,2,1,0:T(4,128)(2,1)S(1)} %bitcast.33, bf16[2,3,3,2,128]{4,3,2,1,0:T(2,128)(2,1)S(1)} %bitcast.36), custom_call_target="tpu_custom_call" | custom-call | flops 8192000 | bytes 617472 | tf_op jit(solution)/shard_map/pallas_call | solution.py:222
  12.4 0.0 copy-start.2
  12.4 0.0 copy-start.3
  12.4 12.2 %all-gather = bf16[4,3,2,32,128]{4,3,2,1,0:T(8,128)(2,1)S(1)} all-gather(bf16[2,3,2,32,128]{4,3,2,1,0:T(8,128)(2,1)S(1)} %get-tuple-element.8), channel_id=2, replica_groups={{0,1},{2,3},{4,5},{6,7},{8,9},{10,11},{12,13},{14,15},{16,17},{18,19},{..., dimensions={0}, use_global_device_ids=true | all-gather | bytes 294912 | tf_op jit(solution)/shard_map/all_gather | solution.py:301
  24.6 0.0 collective-permute-done.first
  24.6 0.0 collective-permute-done.1.second
  24.6 0.0 collective-permute-done.2.third
  24.6 0.0 copy-done.2
  24.6 0.0 copy-done.3
  24.6 1.1 %shard_map.61 = (bf16[2,3,4,32,128]{4,3,2,1,0:T(8,128)(2,1)}, f32[2,64,128]{2,1,0:T(8,128)S(1)}) custom-call(f32[2,3,4,32,128]{4,3,2,1,0:T(8,128)S(1)} %shard_map.59.local, bf16[2,3,3,4,128]{4,3,2,1,0:T(4,128)(2,1)S(1)} %bitcast.34, bf16[2,2,3,2,32,128]{5,4,3,2,1,0:T(8,128)(2,1)S(1)} %bitcast.31, bf16[2,3,2,32,128]{4,3,2,1,0:T(8,128)(2,1)S(1)} %collective-permute-done.first, ...), custom_call_target="tpu_custom_call" | custom-call | flops 4096000 | bytes 1263616 | tf_op jit(solution)/shard_map/pallas_call | solution.py:222
  25.7 9.1 %all-gather.1 = f32[4,64,128]{2,1,0:T(8,128)S(1)} all-gather(f32[2,64,128]{2,1,0:T(8,128)S(1)} %get-tuple-element.13), channel_id=3, replica_groups={{0,1},{2,3},{4,5},{6,7},{8,9},{10,11},{12,13},{14,15},{16,17},{18,19},{..., dimensions={0}, use_global_device_ids=true | all-gather | bytes 196608 | tf_op jit(solution)/shard_map/all_gather | solution.py:234
  34.9 7.2 %all_to_all.5 = bf16[4,2,64,128]{3,2,1,0:T(8,128)(2,1)S(1)} all-to-all(bf16[4,2,64,128]{3,2,1,0:T(8,128)(2,1)S(1)} %broadcast_in_dim.10), channel_id=1, replica_groups={{0,2,4,6},{1,3,5,7},{8,10,12,14},{9,11,13,15},{16,18,20,22},{17,19,21,2..., dimensions={0} | all-to-all | bytes 262144 | tf_op jit(solution)/shard_map/all_to_all | solution.py:248
  42.2 3.7 %collective-permute-start.3 = (bf16[2,64,128]{2,1,0:T(8,128)(2,1)S(1)}, bf16[2,64,128]{2,1,0:T(8,128)(2,1)S(1)}, u32[]{:S(2)}, u32[]{:S(2)}) collective-permute-start(bf16[2,64,128]{2,1,0:T(8,128)(2,1)S(1)} %fusion.8), channel_id=1, source_target_pairs={{0,16},{1,9},{2,18},{3,11},{4,20},{5,13},{6,22},{7,15},{8,0},{9,17... | collective-permute-start | bytes 98312 | tf_op jit(solution)/shard_map/ppermute | solution.py:255
  45.9 4.8 %collective-permute-done.3 = bf16[2,64,128]{2,1,0:T(8,128)(2,1)S(1)} collective-permute-done((bf16[2,64,128]{2,1,0:T(8,128)(2,1)S(1)}, bf16[2,64,128]{2,1,0:T(8,128)(2,1)S(1)}, u32[]{:S(2)}, u32[]{:S(2)}) %collective-permute-start.3) | collective-permute-done | bytes 32800 | tf_op jit(solution)/shard_map/ppermute | solution.py:255
  50.7 4.1 %all-gather.2 = bf16[4,64,128]{2,1,0:T(8,128)(2,1)S(1)} all-gather(bf16[2,64,128]{2,1,0:T(8,128)(2,1)S(1)} %collective-permute-done.3), channel_id=4, replica_groups={{0,1},{2,3},{4,5},{6,7},{8,9},{10,11},{12,13},{14,15},{16,17},{18,19},{..., dimensions={0}, use_global_device_ids=true | all-gather | bytes 98304 | tf_op jit(solution)/shard_map/all_gather | solution.py:255
  54.9 0.7 %fusion.2 = f32[2,1,64,128]{3,2,1,0:T(8,128)} fusion(bf16[4,64,128]{2,1,0:T(8,128)(2,1)S(1)} %all-gather.2, pred[]{:T(512)S(6)} %eq.5, pred[]{:T(512)S(6)} %eq.4, f32[4,2,64,128]{3,2,1,0:T(8,128)S(1)} %convert_element_type.60), kind=kLoop, calls=%fused_computation.8 | loop fusion | flops 262144 | bytes 393218
  (4 shorter events, 0.1 us)
Async XLA Ops:
  0.6 0.9 %copy-start = (bf16[2,3,4,32,1,1,128]{6,3,5,4,2,1,0:T(8,128)(2,1)S(1)}, bf16[2,3,4,32,1,1,128]{6,3,5,4,2,1,0:T(8,128)(2,1)}, u32[]{:S(2)}) copy-start(bf16[2,3,4,32,1,1,128]{6,3,5,4,2,1,0:T(8,128)(2,1)} %param.4) | copy-start | bytes 589828
  1.6 0.7 %copy-start.1 = (bf16[2,4,3,3,1,1,128]{6,1,5,4,3,2,0:T(4,128)(2,1)S(1)}, bf16[2,4,3,3,1,1,128]{6,1,5,4,3,2,0:T(4,128)(2,1)}, u32[]{:S(2)}) copy-start(bf16[2,4,3,3,1,1,128]{6,1,5,4,3,2,0:T(4,128)(2,1)} %param.5) | copy-start | bytes 55300
  2.3 9.4 %copy-start.4 = (bf16[2,2,3,3,1,1,128]{6,1,5,4,3,2,0:T(2,128)(2,1)S(1)}, bf16[2,2,3,3,1,1,128]{6,1,5,4,3,2,0:T(2,128)(2,1)}, u32[]{:S(2)}) copy-start(bf16[2,2,3,3,1,1,128]{6,1,5,4,3,2,0:T(2,128)(2,1)} %param.6) | copy-start | bytes 27652
  2.8 21.8 %collective-permute-start = (bf16[2,3,2,32,128]{4,3,2,1,0:T(8,128)(2,1)S(1)}, bf16[2,3,2,32,128]{4,3,2,1,0:T(8,128)(2,1)S(1)}, u32[]{:S(2)}, u32[]{:S(2)}) collective-permute-start(bf16[2,3,2,32,128]{4,3,2,1,0:T(8,128)(2,1)S(1)} %get-tuple-element.9), channel_id=1, source_target_pairs={{0,23},{1,2},{2,1},{3,4},{4,3},{5,6},{6,5},{7,8},{8,7},{9,10},{10,... | collective-permute-start | bytes 294920 | tf_op jit(solution)/shard_map/ppermute | solution.py:298
  5.1 19.5 %collective-permute-start.1 = (bf16[2,3,2,32,128]{4,3,2,1,0:T(8,128)(2,1)S(1)}, bf16[2,3,2,32,128]{4,3,2,1,0:T(8,128)(2,1)S(1)}, u32[]{:S(2)}, u32[]{:S(2)}) collective-permute-start(bf16[2,3,2,32,128]{4,3,2,1,0:T(8,128)(2,1)S(1)} %get-tuple-element.10), channel_id=1, source_target_pairs={{0,744},{1,745},{2,746},{3,747},{4,748},{5,749},{6,750},{7,751},{8... | collective-permute-start | bytes 294920 | tf_op jit(solution)/shard_map/ppermute | solution.py:299
  9.5 15.1 %collective-permute-start.2 = (bf16[2,3,2,32,128]{4,3,2,1,0:T(8,128)(2,1)S(1)}, bf16[2,3,2,32,128]{4,3,2,1,0:T(8,128)(2,1)S(1)}, u32[]{:S(2)}, u32[]{:S(2)}) collective-permute-start(bf16[2,3,2,32,128]{4,3,2,1,0:T(8,128)(2,1)S(1)} %get-tuple-element.11), channel_id=1, source_target_pairs={{0,24},{1,25},{2,26},{3,27},{4,28},{5,29},{6,30},{7,31},{8,32},{9,... | collective-permute-start | bytes 294920 | tf_op jit(solution)/shard_map/ppermute | solution.py:300
  12.4 12.2 %copy-start.2 = (bf16[2,4,3,3,1,1,128]{6,1,5,4,3,2,0:T(4,128)(2,1)S(1)}, bf16[2,4,3,3,1,1,128]{6,1,5,4,3,2,0:T(4,128)(2,1)}, u32[]{:S(2)}) copy-start(bf16[2,4,3,3,1,1,128]{6,1,5,4,3,2,0:T(4,128)(2,1)} %param.5) | copy-start | bytes 55300
  12.4 12.2 %copy-start.3 = (bf16[2,3,64,1,1,128]{5,2,4,3,1,0:T(8,128)(2,1)S(1)}, bf16[2,3,64,1,1,128]{5,2,4,3,1,0:T(8,128)(2,1)}, u32[]{:S(2)}) copy-start(bf16[2,3,64,1,1,128]{5,2,4,3,1,0:T(8,128)(2,1)} %param.7) | copy-start | bytes 294916
  42.2 8.6 %collective-permute-start.3 = (bf16[2,64,128]{2,1,0:T(8,128)(2,1)S(1)}, bf16[2,64,128]{2,1,0:T(8,128)(2,1)S(1)}, u32[]{:S(2)}, u32[]{:S(2)}) collective-permute-start(bf16[2,64,128]{2,1,0:T(8,128)(2,1)S(1)} %fusion.8), channel_id=1, source_target_pairs={{0,16},{1,9},{2,18},{3,11},{4,20},{5,13},{6,22},{7,15},{8,0},{9,17... | collective-permute-start | bytes 98312 | tf_op jit(solution)/shard_map/ppermute | solution.py:255

commit v3 on v2

--- a/solution.py
+++ b/solution.py
@@ -9,6 +9,7 @@
 
 KAPPA = 0.125
 ROWS = 16
+LINK_ROWS = 72
 F32 = jnp.float32
 BF16 = jnp.bfloat16
 
@@ -57,6 +58,28 @@
     return [
         [(ref[0, c, s, rows, :].astype(F32), ref[1, c, s, rows, :].astype(F32)) for s in range(spins)]
         for c in range(3)
+    ]
+
+
+class Field:
+    def __init__(self, packed):
+        self.packed, self.shape = packed, (2, 3, 4, (packed.shape[0] - LINK_ROWS) // 24, packed.shape[1])
+
+    def __getitem__(self, at):
+        q, c, s, rows, _ = at
+        return self.packed[pl.ds(((q * 3 + c) * 4 + s) * self.shape[3] + rows.start, rows.size), :]
+
+
+def load_links(packed, *directions):
+    block = packed[pl.ds(packed.shape[0] - LINK_ROWS, LINK_ROWS), :].astype(F32)
+
+    def row(q, a, b, direction):
+        at = ((q * 3 + a) * 3 + b) * 4 + direction
+        return block[at : at + 1, :]
+
+    return [
+        [[(row(0, a, b, direction), row(1, a, b, direction)) for b in range(3)] for a in range(3)]
+        for direction in directions
     ]
 
 
@@ -91,17 +114,10 @@
     return out
 
 
-def edge_kernel(ta_size, src_hbm, links_hbm, to_core, to_first, to_second, to_third, src, links, sems):
-    copies = [
-        pltpu.make_async_copy(src_hbm, src, sems.at[0]),
-        pltpu.make_async_copy(links_hbm, links, sems.at[1]),
-    ]
-    for copy in copies:
-        copy.start()
-    for copy in copies:
-        copy.wait()
+def edge_kernel(ta_size, packed, to_core, to_first, to_second, to_third):
+    src = Field(packed)
     columns = src.shape[3]
-    link_z, link_t = load_matrix(links, 2), load_matrix(links, 3)
+    link_z, link_t = load_links(packed, 2, 3)
     me = lax.axis_index("ta")
     even_z = lax.axis_index("sa") % 2 == 0
     even_t = me % 2 == 0
@@ -134,9 +150,56 @@
     return jnp.where(lane % 8 == 0, pltpu.roll(x, 121, 1), pltpu.roll(x, 1, 1))
 
 
-def local_kernel(src, links, clover, out):
+def add_to(hop, a, values):
+    for s, v in enumerate(values):
+        hop[a][s] = v if hop[a][s] is None else add(hop[a][s], v)
+
+
+def place_on_mesh(ta_size):
+    me, core = lax.axis_index("ta"), lax.axis_index("sa") % 2
+    ahead_sign = jnp.where(me == ta_size - 1, -1.0, 1.0).astype(F32)
+    behind_sign = jnp.where(me == 0, -1.0, 1.0).astype(F32)
+    return core, me % 2, me >= ta_size - 2, ahead_sign, behind_sign
+
+
+def chosen_matrix(first, a, b):
+    return [[tuple(jnp.where(first, p, q) for p, q in zip(v, w)) for v, w in zip(x, y)] for x, y in zip(a, b)]
+
+
+def add_swapped(hop, link, part, forward, turn, forward_sign=None, backward_sign=None):
+    for a in range(3):
+        upper, signed = [], []
+        for s in range(2):
+            w, g = color_row(link, part, a, s, False), part[a][s]
+            if forward_sign is not None:
+                w = (w[0] * forward_sign, w[1] * forward_sign)
+                g = (g[0] * backward_sign, g[1] * backward_sign)
+            upper.append(tuple(jnp.where(forward, p, q) for p, q in zip(w, g)))
+            signed.append(tuple(jnp.where(forward, -p, q) for p, q in zip(w, g)))
+        add_to(hop, a, upper + turn(signed))
+
+
+def turned_z(w):
+    return spin_dagger(2, w)
+
+
+def turned_t(w):
+    return spin_dagger(3, w)
+
+
+def turned_either(along_t, w):
+    return [
+        tuple(jnp.where(along_t, p, q) for p, q in zip(v, u)) for v, u in zip(turned_t(w), turned_z(w))
+    ]
+
+
+def local_kernel(ta_size, packed, clover, cores, first, second, out):
+    src = Field(packed)
     columns = src.shape[3]
-    link = {0: load_matrix(links, 0), 1: load_matrix(links, 1)}
+    core, odd_t, last, ahead_sign, behind_sign = place_on_mesh(ta_size)
+    link = load_links(packed, 0, 1, 2, 3)
+    link_first = chosen_matrix(last, link[3], link[2])
+    forward_first = jnp.where(last, 1 - odd_t, core) == 1
     clov = [load_matrix(clover, 0), load_matrix(clover, 1)]
     for at in range(0, columns, ROWS):
         rows = pl.ds(at, ROWS)
@@ -159,9 +222,10 @@
                     for s in range(2)
                 ]
                 upper = [add(w[s], g[s]) for s in range(2)]
-                lower = spin_dagger(direction, [sub(g[s], w[s]) for s in range(2)])
-                for s, v in enumerate(upper + lower):
-                    hop[a][s] = v if hop[a][s] is None else add(hop[a][s], v)
+                add_to(hop, a, upper + spin_dagger(direction, [sub(g[s], w[s]) for s in range(2)]))
+        add_swapped(hop, link[2], load_field(cores.at[1 - core], rows, 2), core == 0, turned_z)
+        add_swapped(hop, link_first, load_field(first, rows, 2), forward_first, functools.partial(turned_either, last))
+        add_swapped(hop, link[3], load_field(second, rows, 2), odd_t == 1, turned_t, ahead_sign, behind_sign)
         for a in range(3):
             for s in range(4):
                 own = add(field[a][s], color_row(clov[s // 2], field, a, s, False))
@@ -169,40 +233,21 @@
                     out[q, a, s, rows, :] = own[q] - KAPPA * hop[a][s][q]
 
 
-def chosen(first, a, b):
-    return [[tuple(jnp.where(first, p, q) for p, q in zip(v, w)) for v, w in zip(x, y)] for x, y in zip(a, b)]
-
-
-def finish_kernel(ta_size, local, links, cores, first, second, third, vectors, result, partial):
+def finish_kernel(ta_size, local, packed, third, vectors, result, partial):
     columns = local.shape[3]
-    me = lax.axis_index("ta")
-    core = lax.axis_index("sa") % 2
-    even_z = core == 0
-    even_t = me % 2 == 0
-    last = me >= ta_size - 2
-    ahead_sign = jnp.where(me == ta_size - 1, -1.0, 1.0).astype(F32)
-    behind_sign = jnp.where(me == 0, -1.0, 1.0).astype(F32)
-    link_z = load_matrix(links, 2)
-    link_t = [[(m[0] * ahead_sign, m[1] * ahead_sign) for m in row] for row in load_matrix(links, 3)]
+    core, odd_t, last, _, _ = place_on_mesh(ta_size)
+    link = chosen_matrix(last, *load_links(packed, 2, 3))
+    forward = jnp.where(last, core, 1 - odd_t) == 1
+    turn = functools.partial(turned_either, jnp.logical_not(last))
     for at in range(0, columns, ROWS):
         rows = pl.ds(at, ROWS)
-        one, three = load_field(first, rows, 2), load_field(third, rows, 2)
-        near, far = load_field(cores.at[1 - core], rows, 2), chosen(last, three, one)
-        from_z, back_z = chosen(even_z, near, far), chosen(even_z, far, near)
-        near, far = chosen(last, one, three), load_field(second, rows, 2)
-        from_t, back_t = chosen(even_t, near, far), chosen(even_t, far, near)
+        hop = [[None] * 4 for _ in range(3)]
+        add_swapped(hop, link, load_field(third, rows, 2), forward, turn)
         for a in range(3):
-            wz = [color_row(link_z, from_z, a, s, False) for s in range(2)]
-            wt = [color_row(link_t, from_t, a, s, False) for s in range(2)]
-            gz_now = back_z[a]
-            gt_now = [(v[0] * behind_sign, v[1] * behind_sign) for v in back_t[a]]
-            lower_z = spin_dagger(2, [sub(gz_now[s], wz[s]) for s in range(2)])
-            for s in range(2):
-                upper = add(add(wz[s], gz_now[s]), add(wt[s], gt_now[s]))
-                lower = add(lower_z[s], sub(gt_now[s], wt[s]))
+            for s in range(4):
                 for q in range(2):
-                    result[q, a, s, rows, :] = (local[q, a, s, rows, :] - KAPPA * upper[q]).astype(BF16)
-                    result[q, a, s + 2, rows, :] = (local[q, a, s + 2, rows, :] - KAPPA * lower[q]).astype(BF16)
+                    value = local[q, a, s, rows, :] - KAPPA * hop[a][s][q]
+                    result[q, a, s, rows, :] = value.astype(BF16)
     total = None
     contract = (((1,), (1,)), ((), ()))
     for c in range(3):
@@ -214,6 +259,10 @@
             term = lax.dot_general(jnp.concatenate(left, axis=0), right, contract, preferred_element_type=F32)
             total = term if total is None else total + term
     partial[...] = total.reshape(partial.shape)
+
+
+def copy_kernel(src, out):
+    out[...] = src[...]
 
 
 def call(body, outs, operands, flops, in_specs=None, scratch_shapes=()):
@@ -272,17 +321,12 @@
     half_shape = jax.ShapeDtypeStruct((2, 3, 2, columns, sites), BF16)
     points = columns * sites
 
+    packed = jnp.concatenate([src.reshape(-1, sites), links.reshape(-1, sites)])
     to_core, to_first, to_second, to_third = call(
         functools.partial(edge_kernel, ta),
         [half_shape] * 4,
-        (src, links),
+        (packed,),
         500 * points,
-        in_specs=[pl.BlockSpec(memory_space=pl.ANY)] * 2,
-        scratch_shapes=[
-            pltpu.VMEM(src.shape, BF16),
-            pltpu.VMEM(links.shape, BF16),
-            pltpu.SemaphoreType.DMA((2,)),
-        ],
     )
 
     def place(t, z):
@@ -300,10 +344,10 @@
     third = lax.ppermute(to_third, ("ta", "sa"), along_t(most, 0) + along_z(rest))
     cores = lax.all_gather(to_core, "sa", axis_index_groups=[[i, i + 1] for i in range(0, sa, 2)])
     (local,) = call(
-        local_kernel,
+        functools.partial(local_kernel, ta),
         [jax.ShapeDtypeStruct((2, 3, 4, columns, sites), F32)],
-        (src, links, clov),
-        2000 * points,
+        (packed, clov, cores, first, second),
+        2500 * points,
     )
     result, partial = call(
         functools.partial(finish_kernel, ta),
@@ -311,10 +355,11 @@
             jax.ShapeDtypeStruct((2, 3, 4, columns, sites), BF16),
             jax.ShapeDtypeStruct((2, vectors.shape[2], 4 * columns), F32),
         ],
-        (local, links, cores, first, second, third, vectors),
-        1000 * points,
+        (local, packed, third, vectors),
+        500 * points,
     )
     perambulator = sum_over_blocks(partial, sa)
+    (result,) = call(copy_kernel, [jax.ShapeDtypeStruct(result.shape, BF16)], (result,), 2000 * points)
     return result.reshape(source_field.shape), perambulator[:, None]
 
 

time: 55.9 us -> 54.2 us (0.970)
  the two profiles are of different devices: /device:TPU:241 before, /device:TPU:1 now
where the time goes in v3:
time: 54.2 us; the launch traced here: 53.7 us
  blocking collectives  24.7 us (46%)
  starting transfers between devices  20.9 us (39%)
  waiting for transfers between devices  3.18 us (6%)
  Pallas kernels  2.37 us (4%)
  other arithmetic  1.68 us (3%)
  between operations  0.78 us (1%)
    all_gather x1, blocking collectives, shards(): lax.all_gather(to_core, 'sa', axis_index_groups=[[i, i + 1] for i in rang...  10 us
    ppermute x1, starting transfers between devices, shards(): second = lax.ppermute(to_second, ('ta', 'sa'), along_t(range(ta), 1))  9.82 us
    all_to_all x1, blocking collectives, sum_over_blocks(): lax.all_to_all(jnp.broadcast_to(s[None], (4,) + s.shape), 'sa', 0, 0, axi...  7.23 us
    ppermute x1, starting transfers between devices, sum_over_blocks(): lax.ppermute(s, 'sa', pairs)  4.66 us
    ppermute x1, starting transfers between devices, shards(): lax.ppermute(to_first, ('ta', 'sa'), along_z(most) + along_t(rest, 0))  4.51 us
    all_gather x1, blocking collectives, sum_over_blocks(): lax.all_gather(lax.ppermute(s, 'sa', pairs), 'sa', axis_index_groups=cores)  4.13 us
    all_gather x1, blocking collectives, gathered_sum(): both = lax.all_gather(x, 'sa', axis_index_groups=groups).astype(F32)  3.35 us
    ppermute x1, waiting for transfers between devices, sum_over_blocks(): lax.ppermute(s, 'sa', pairs)  3.17 us
  transfers between devices with their start and end apart: 4, of which 1 were waited for; matrix products, arithmetic and copies ran while one was open for 0% of the time, Pallas kernels for 3%

profile of v3, /device:TPU:1, one launch (start us, length us, event | category | flops | bytes accessed | tf_op | source)
XLA Modules:
  0.0 53.7 jit_solution(9708642554486697249)
XLA Ops:
  0.6 1.0 %pad_maximum_fusion.packed = bf16[840,128]{1,0:T(8,128)(2,1)S(1)} fusion(bf16[72,128]{1,0:T(8,128)(2,1)} %bitcast.36, bf16[768,128]{1,0:T(8,128)(2,1)} %bitcast.35), kind=kLoop, calls=%fused_computation | loop fusion | flops 430080 | bytes 430080 | tf_op jit(solution)/shard_map/concatenate | solution.py:324
  1.6 0.3 shard_map.59
  1.9 4.5 %collective-permute-start = (bf16[2,3,2,32,128]{4,3,2,1,0:T(8,128)(2,1)S(1)}, bf16[2,3,2,32,128]{4,3,2,1,0:T(8,128)(2,1)S(1)}, u32[]{:S(2)}, u32[]{:S(2)}) collective-permute-start(bf16[2,3,2,32,128]{4,3,2,1,0:T(8,128)(2,1)S(1)} %get-tuple-element.9), channel_id=1, source_target_pairs={{0,23},{1,2},{2,1},{3,4},{4,3},{5,6},{6,5},{7,8},{8,7},{9,10},{10,... | collective-permute-start | bytes 294920 | tf_op jit(solution)/shard_map/ppermute | solution.py:342
  6.4 9.8 %collective-permute-start.1 = (bf16[2,3,2,32,128]{4,3,2,1,0:T(8,128)(2,1)S(1)}, bf16[2,3,2,32,128]{4,3,2,1,0:T(8,128)(2,1)S(1)}, u32[]{:S(2)}, u32[]{:S(2)}) collective-permute-start(bf16[2,3,2,32,128]{4,3,2,1,0:T(8,128)(2,1)S(1)} %get-tuple-element.10), channel_id=1, source_target_pairs={{0,744},{1,745},{2,746},{3,747},{4,748},{5,749},{6,750},{7,751},{8... | collective-permute-start | bytes 294920 | tf_op jit(solution)/shard_map/ppermute | solution.py:343
  16.2 1.9 %collective-permute-start.2 = (bf16[2,3,2,32,128]{4,3,2,1,0:T(8,128)(2,1)S(1)}, bf16[2,3,2,32,128]{4,3,2,1,0:T(8,128)(2,1)S(1)}, u32[]{:S(2)}, u32[]{:S(2)}) collective-permute-start(bf16[2,3,2,32,128]{4,3,2,1,0:T(8,128)(2,1)S(1)} %get-tuple-element.11), channel_id=1, source_target_pairs={{0,24},{1,25},{2,26},{3,27},{4,28},{5,29},{6,30},{7,31},{8,32},{9,... | collective-permute-start | bytes 294920 | tf_op jit(solution)/shard_map/ppermute | solution.py:344
  18.1 0.0 copy-start.1
  18.1 10.0 %all-gather = bf16[4,3,2,32,128]{4,3,2,1,0:T(8,128)(2,1)S(1)} all-gather(bf16[2,3,2,32,128]{4,3,2,1,0:T(8,128)(2,1)S(1)} %get-tuple-element.8), channel_id=2, replica_groups={{0,1},{2,3},{4,5},{6,7},{8,9},{10,11},{12,13},{14,15},{16,17},{18,19},{..., dimensions={0}, use_global_device_ids=true | all-gather | bytes 294912 | tf_op jit(solution)/shard_map/all_gather | solution.py:345
  28.1 0.0 collective-permute-done.first
  28.2 0.0 collective-permute-done.1.second
  28.2 0.0 copy-done.1
  28.2 0.0 copy-start
  28.2 1.0 %shard_map.60.local = f32[2,3,4,32,128]{4,3,2,1,0:T(8,128)S(1)} custom-call(bf16[840,128]{1,0:T(8,128)(2,1)S(1)} %pad_maximum_fusion.packed, bf16[2,3,3,2,128]{4,3,2,1,0:T(2,128)(2,1)S(1)} %bitcast.33, bf16[2,2,3,2,32,128]{5,4,3,2,1,0:T(8,128)(2,1)S(1)} %bitcast.31, bf16[2,3,2,32,128]{4,3,2,1,0:T(8,128)(2,1)S(1)} %collective-permute-done.first, ...), custom_call_target="tpu_custom_call" | custom-call | flops 10240000 | bytes 1010688 | tf_op jit(solution)/shard_map/pallas_call | solution.py:271
  29.2 0.0 collective-permute-done.2.third
  29.2 0.0 copy-done
  29.2 0.4 shard_map.61
  29.6 3.4 %all-gather.1 = f32[4,64,128]{2,1,0:T(8,128)S(1)} all-gather(f32[2,64,128]{2,1,0:T(8,128)S(1)} %get-tuple-element.13), channel_id=3, replica_groups={{0,1},{2,3},{4,5},{6,7},{8,9},{10,11},{12,13},{14,15},{16,17},{18,19},{..., dimensions={0}, use_global_device_ids=true | all-gather | bytes 196608 | tf_op jit(solution)/shard_map/all_gather | solution.py:283
  33.0 7.2 %all_to_all.5 = bf16[4,2,64,128]{3,2,1,0:T(8,128)(2,1)S(1)} all-to-all(bf16[4,2,64,128]{3,2,1,0:T(8,128)(2,1)S(1)} %broadcast_in_dim.10), channel_id=1, replica_groups={{0,2,4,6},{1,3,5,7},{8,10,12,14},{9,11,13,15},{16,18,20,22},{17,19,21,2..., dimensions={0} | all-to-all | bytes 262144 | tf_op jit(solution)/shard_map/all_to_all | solution.py:297
  40.3 4.7 %collective-permute-start.3 = (bf16[2,64,128]{2,1,0:T(8,128)(2,1)S(1)}, bf16[2,64,128]{2,1,0:T(8,128)(2,1)S(1)}, u32[]{:S(2)}, u32[]{:S(2)}) collective-permute-start(bf16[2,64,128]{2,1,0:T(8,128)(2,1)S(1)} %fusion.8), channel_id=1, source_target_pairs={{0,16},{1,9},{2,18},{3,11},{4,20},{5,13},{6,22},{7,15},{8,0},{9,17... | collective-permute-start | bytes 98312 | tf_op jit(solution)/shard_map/ppermute | solution.py:304
  45.0 0.7 %shard_map.62 = bf16[2,3,4,32,128]{4,3,2,1,0:T(8,128)(2,1)} custom-call(bf16[2,3,4,32,128]{4,3,2,1,0:T(8,128)(2,1)S(1)} %get-tuple-element.12.src), custom_call_target="tpu_custom_call" | custom-call | flops 8192000 | bytes 393216 | tf_op jit(solution)/shard_map/pallas_call | solution.py:271
  45.7 3.2 %collective-permute-done.3 = bf16[2,64,128]{2,1,0:T(8,128)(2,1)S(1)} collective-permute-done((bf16[2,64,128]{2,1,0:T(8,128)(2,1)S(1)}, bf16[2,64,128]{2,1,0:T(8,128)(2,1)S(1)}, u32[]{:S(2)}, u32[]{:S(2)}) %collective-permute-start.3) | collective-permute-done | bytes 32800 | tf_op jit(solution)/shard_map/ppermute | solution.py:304
  48.9 4.1 %all-gather.2 = bf16[4,64,128]{2,1,0:T(8,128)(2,1)S(1)} all-gather(bf16[2,64,128]{2,1,0:T(8,128)(2,1)S(1)} %collective-permute-done.3), channel_id=4, replica_groups={{0,1},{2,3},{4,5},{6,7},{8,9},{10,11},{12,13},{14,15},{16,17},{18,19},{..., dimensions={0}, use_global_device_ids=true | all-gather | bytes 98304 | tf_op jit(solution)/shard_map/all_gather | solution.py:304
  53.0 0.7 %fusion.2 = f32[2,1,64,128]{3,2,1,0:T(8,128)} fusion(bf16[4,64,128]{2,1,0:T(8,128)(2,1)S(1)} %all-gather.2, pred[]{:T(512)S(6)} %eq.5, pred[]{:T(512)S(6)} %eq.4, f32[4,2,64,128]{3,2,1,0:T(8,128)S(1)} %convert_element_type.60), kind=kLoop, calls=%fused_computation.9 | loop fusion | flops 262144 | bytes 393218
  (4 shorter events, 0.1 us)
Async XLA Ops:
  1.9 26.3 %collective-permute-start = (bf16[2,3,2,32,128]{4,3,2,1,0:T(8,128)(2,1)S(1)}, bf16[2,3,2,32,128]{4,3,2,1,0:T(8,128)(2,1)S(1)}, u32[]{:S(2)}, u32[]{:S(2)}) collective-permute-start(bf16[2,3,2,32,128]{4,3,2,1,0:T(8,128)(2,1)S(1)} %get-tuple-element.9), channel_id=1, source_target_pairs={{0,23},{1,2},{2,1},{3,4},{4,3},{5,6},{6,5},{7,8},{8,7},{9,10},{10,... | collective-permute-start | bytes 294920 | tf_op jit(solution)/shard_map/ppermute | solution.py:342
  6.4 21.8 %collective-permute-start.1 = (bf16[2,3,2,32,128]{4,3,2,1,0:T(8,128)(2,1)S(1)}, bf16[2,3,2,32,128]{4,3,2,1,0:T(8,128)(2,1)S(1)}, u32[]{:S(2)}, u32[]{:S(2)}) collective-permute-start(bf16[2,3,2,32,128]{4,3,2,1,0:T(8,128)(2,1)S(1)} %get-tuple-element.10), channel_id=1, source_target_pairs={{0,744},{1,745},{2,746},{3,747},{4,748},{5,749},{6,750},{7,751},{8... | collective-permute-start | bytes 294920 | tf_op jit(solution)/shard_map/ppermute | solution.py:343
  16.2 13.0 %collective-permute-start.2 = (bf16[2,3,2,32,128]{4,3,2,1,0:T(8,128)(2,1)S(1)}, bf16[2,3,2,32,128]{4,3,2,1,0:T(8,128)(2,1)S(1)}, u32[]{:S(2)}, u32[]{:S(2)}) collective-permute-start(bf16[2,3,2,32,128]{4,3,2,1,0:T(8,128)(2,1)S(1)} %get-tuple-element.11), channel_id=1, source_target_pairs={{0,24},{1,25},{2,26},{3,27},{4,28},{5,29},{6,30},{7,31},{8,32},{9,... | collective-permute-start | bytes 294920 | tf_op jit(solution)/shard_map/ppermute | solution.py:344
  18.1 10.0 %copy-start.1 = (bf16[2,2,3,3,1,1,128]{6,1,5,4,3,2,0:T(2,128)(2,1)S(1)}, bf16[2,2,3,3,1,1,128]{6,1,5,4,3,2,0:T(2,128)(2,1)}, u32[]{:S(2)}) copy-start(bf16[2,2,3,3,1,1,128]{6,1,5,4,3,2,0:T(2,128)(2,1)} %param.6) | copy-start | bytes 27652
  28.2 1.1 %copy-start = (bf16[2,3,64,1,1,128]{5,2,4,3,1,0:T(8,128)(2,1)S(1)}, bf16[2,3,64,1,1,128]{5,2,4,3,1,0:T(8,128)(2,1)}, u32[]{:S(2)}) copy-start(bf16[2,3,64,1,1,128]{5,2,4,3,1,0:T(8,128)(2,1)} %param.7) | copy-start | bytes 294916
  40.3 8.6 %collective-permute-start.3 = (bf16[2,64,128]{2,1,0:T(8,128)(2,1)S(1)}, bf16[2,64,128]{2,1,0:T(8,128)(2,1)S(1)}, u32[]{:S(2)}, u32[]{:S(2)}) collective-permute-start(bf16[2,64,128]{2,1,0:T(8,128)(2,1)S(1)} %fusion.8), channel_id=1, source_target_pairs={{0,16},{1,9},{2,18},{3,11},{4,20},{5,13},{6,22},{7,15},{8,0},{9,17... | collective-permute-start | bytes 98312 | tf_op jit(solution)/shard_map/ppermute | solution.py:304

commit v4 on v3

--- a/solution.py
+++ b/solution.py
@@ -114,6 +114,10 @@
     return out
 
 
+def late_slabs(me, ta_size):
+    return me >= ta_size - 4, (me == ta_size - 3) | (me == ta_size - 2)
+
+
 def edge_kernel(ta_size, packed, to_core, to_first, to_second, to_third):
     src = Field(packed)
     columns = src.shape[3]
@@ -121,7 +125,7 @@
     me = lax.axis_index("ta")
     even_z = lax.axis_index("sa") % 2 == 0
     even_t = me % 2 == 0
-    last = me >= ta_size - 2
+    late, middle = late_slabs(me, ta_size)
     for at in range(0, columns, ROWS):
         rows = pl.ds(at, ROWS)
         field = load_field(src, rows, 4)
@@ -136,9 +140,10 @@
                     chip = jnp.where(even_z, minus_z[a][s][q], back_z[q])
                     even = jnp.where(even_t, back_t[q], minus_t[a][s][q])
                     odd = jnp.where(even_t, minus_t[a][s][q], back_t[q])
-                    to_first[q, a, s, rows, :] = jnp.where(last, even, chip).astype(BF16)
-                    to_second[q, a, s, rows, :] = odd.astype(BF16)
-                    to_third[q, a, s, rows, :] = jnp.where(last, chip, even).astype(BF16)
+                    to_first[q, a, s, rows, :] = jnp.where(late, even, chip).astype(BF16)
+                    to_second[q, a, s, rows, :] = jnp.where(middle, chip, odd).astype(BF16)
+                    third = jnp.where(middle, odd, jnp.where(late, chip, even))
+                    to_third[q, a, s, rows, :] = third.astype(BF16)
 
 
 def shift_sites(x, direction, ahead):
@@ -159,7 +164,7 @@
     me, core = lax.axis_index("ta"), lax.axis_index("sa") % 2
     ahead_sign = jnp.where(me == ta_size - 1, -1.0, 1.0).astype(F32)
     behind_sign = jnp.where(me == 0, -1.0, 1.0).astype(F32)
-    return core, me % 2, me >= ta_size - 2, ahead_sign, behind_sign
+    return core, me % 2, *late_slabs(me, ta_size), ahead_sign, behind_sign
 
 
 def chosen_matrix(first, a, b):
@@ -196,10 +201,14 @@
 def local_kernel(ta_size, packed, clover, cores, first, second, out):
     src = Field(packed)
     columns = src.shape[3]
-    core, odd_t, last, ahead_sign, behind_sign = place_on_mesh(ta_size)
+    core, odd_t, late, middle, ahead_sign, behind_sign = place_on_mesh(ta_size)
     link = load_links(packed, 0, 1, 2, 3)
-    link_first = chosen_matrix(last, link[3], link[2])
-    forward_first = jnp.where(last, 1 - odd_t, core) == 1
+    link_first = chosen_matrix(late, link[3], link[2])
+    link_second = chosen_matrix(middle, link[2], link[3])
+    forward_first = jnp.where(late, 1 - odd_t, core) == 1
+    forward_second = jnp.where(middle, core, odd_t) == 1
+    turn_first = functools.partial(turned_either, late)
+    turn_second = functools.partial(turned_either, jnp.logical_not(middle))
     clov = [load_matrix(clover, 0), load_matrix(clover, 1)]
     for at in range(0, columns, ROWS):
         rows = pl.ds(at, ROWS)
@@ -224,8 +233,9 @@
                 upper = [add(w[s], g[s]) for s in range(2)]
                 add_to(hop, a, upper + spin_dagger(direction, [sub(g[s], w[s]) for s in range(2)]))
         add_swapped(hop, link[2], load_field(cores.at[1 - core], rows, 2), core == 0, turned_z)
-        add_swapped(hop, link_first, load_field(first, rows, 2), forward_first, functools.partial(turned_either, last))
-        add_swapped(hop, link[3], load_field(second, rows, 2), odd_t == 1, turned_t, ahead_sign, behind_sign)
+        add_swapped(hop, link_first, load_field(first, rows, 2), forward_first, turn_first)
+        part = load_field(second, rows, 2)
+        add_swapped(hop, link_second, part, forward_second, turn_second, ahead_sign, behind_sign)
         for a in range(3):
             for s in range(4):
                 own = add(field[a][s], color_row(clov[s // 2], field, a, s, False))
@@ -235,10 +245,11 @@
 
 def finish_kernel(ta_size, local, packed, third, vectors, result, partial):
     columns = local.shape[3]
-    core, odd_t, last, _, _ = place_on_mesh(ta_size)
-    link = chosen_matrix(last, *load_links(packed, 2, 3))
-    forward = jnp.where(last, core, 1 - odd_t) == 1
-    turn = functools.partial(turned_either, jnp.logical_not(last))
+    core, odd_t, late, middle, _, _ = place_on_mesh(ta_size)
+    along_z = late & jnp.logical_not(middle)
+    link = chosen_matrix(along_z, *load_links(packed, 2, 3))
+    forward = jnp.where(middle, odd_t, jnp.where(late, core, 1 - odd_t)) == 1
+    turn = functools.partial(turned_either, jnp.logical_not(along_z))
     for at in range(0, columns, ROWS):
         rows = pl.ds(at, ROWS)
         hop = [[None] * 4 for _ in range(3)]
@@ -284,7 +295,7 @@
     return lax.reduce_precision(both[0] + both[1], 8, 7).astype(BF16)
 
 
-def sum_over_blocks(partial, size):
+def sum_over_blocks(partial, result, size):
     plane = 8
     planes = size // plane
     cores = [[i, i + 1] for i in range(0, size, 2)]
@@ -292,22 +303,25 @@
     even = [[z + 4 * p + c, z + 4 * p + 2 + c] for z in starts for p in range(2) for c in range(2)]
     odd = [[z + 2 + c, z + 4 + c] for z in starts for c in range(2)]
     odd += [[z + c, z + 6 + c] for z in starts for c in range(2)]
+    row = [[z + 2 * x + c for x in range(4)] for z in starts for c in range(2)]
     s = gathered_sum(partial, cores)
-    row = [[z + 2 * x + c for x in range(4)] for z in starts for c in range(2)]
-    four = lax.all_to_all(jnp.broadcast_to(s[None], (4,) + s.shape), "sa", 0, 0, axis_index_groups=row).astype(F32)
-    s = lax.reduce_precision((four[0] + four[1]) + (four[2] + four[3]), 8, 7).astype(BF16)
     pairs = []
     for i in range(size):
         z, r = divmod(i, plane)
         step = 1 if i % 2 else planes - 1
         pairs.append((i, ((z + step) % planes) * plane + r))
-    other = lax.all_gather(lax.ppermute(s, "sa", pairs), "sa", axis_index_groups=cores)
+    other = lax.ppermute(s, "sa", pairs)
+    (result,) = call(copy_kernel, [jax.ShapeDtypeStruct(result.shape, BF16)], (result,), result.size)
+    other, result = lax.optimization_barrier((other, result))
+    other = lax.all_gather(other, "sa", axis_index_groups=cores)
     z = lax.axis_index("sa") // plane
     own, nxt, last = s.astype(F32), other[0].astype(F32), other[1].astype(F32)
     first = jnp.where(z == 0, own, jnp.where(z == 1, last, nxt))
     second = jnp.where(z == 0, nxt, jnp.where(z == 1, own, last))
     third = jnp.where(z == 0, last, jnp.where(z == 1, nxt, own))
-    return first + second + third
+    s = lax.reduce_precision(first + second + third, 8, 7).astype(BF16)
+    four = lax.all_to_all(jnp.broadcast_to(s[None], (4,) + s.shape), "sa", 0, 0, axis_index_groups=row).astype(F32)
+    return (four[0] + four[1]) + (four[2] + four[3]), result
 
 
 def shards(source_field, gauge_links, clover, eigenvectors):
@@ -338,10 +352,11 @@
     def along_t(slabs, parity):
         return [(place(t, z), place(t + (1 if t % 2 == parity else -1), z)) for t in slabs for z in range(sa)]
 
-    most, rest = range(ta - 2), range(ta - 2, ta)
-    first = lax.ppermute(to_first, ("ta", "sa"), along_z(most) + along_t(rest, 0))
-    second = lax.ppermute(to_second, ("ta", "sa"), along_t(range(ta), 1))
-    third = lax.ppermute(to_third, ("ta", "sa"), along_t(most, 0) + along_z(rest))
+    early, late, middle, ends = range(ta - 4), range(ta - 4, ta), (ta - 3, ta - 2), (ta - 4, ta - 1)
+    others = [t for t in range(ta) if t not in middle]
+    first = lax.ppermute(to_first, ("ta", "sa"), along_z(early) + along_t(late, 0))
+    second = lax.ppermute(to_second, ("ta", "sa"), along_t(others, 1) + along_z(middle))
+    third = lax.ppermute(to_third, ("ta", "sa"), along_t(early, 0) + along_z(ends) + along_t(middle, 1))
     cores = lax.all_gather(to_core, "sa", axis_index_groups=[[i, i + 1] for i in range(0, sa, 2)])
     (local,) = call(
         functools.partial(local_kernel, ta),
@@ -358,8 +373,7 @@
         (local, packed, third, vectors),
         500 * points,
     )
-    perambulator = sum_over_blocks(partial, sa)
-    (result,) = call(copy_kernel, [jax.ShapeDtypeStruct(result.shape, BF16)], (result,), 2000 * points)
+    perambulator, result = sum_over_blocks(partial, result, sa)
     return result.reshape(source_field.shape), perambulator[:, None]
 
 

time: 54.2 us -> 53 us (0.978)
  waiting for transfers between devices: 3.18 us -> 5.15 us
  blocking collectives: 24.7 us -> 23.1 us
  starting transfers between devices: 20.9 us -> 19.5 us
    ppermute x4, waiting for transfers between devices: 3.18 us -> 5.15 us  [the longest x1 5.14 us: sum_over_blocks(): other = lax.ppermute(s, 'sa', pairs)]
    all_gather x1, blocking collectives: 4.13 us -> 2.47 us  [sum_over_blocks(): other = lax.all_gather(other, 'sa', axis_index_groups=cores)]
    ppermute x4, starting transfers between devices: 20.9 us -> 19.5 us  [the longest x1 9.82 us: shards(): lax.ppermute(to_second, ('ta', 'sa'), along_t(others, 1) + along_z(middle))]
    unnamed x1 -> x0, other arithmetic: 0.67 us -> none
    add x0 -> x1, other arithmetic: none -> 0.65 us  [sum_over_blocks(): return (four[0] + four[1] + (four[2] + four[3]), result)]
where the time goes in v4:
time: 53 us; the launch traced here: 52.6 us
  blocking collectives  23.1 us (44%)
  starting transfers between devices  19.5 us (37%)
  waiting for transfers between devices  5.15 us (10%)
  Pallas kernels  2.41 us (5%)
  other arithmetic  1.67 us (3%)
  between operations  0.77 us (1%)
    all_gather x1, blocking collectives, shards(): lax.all_gather(to_core, 'sa', axis_index_groups=[[i, i + 1] for i in rang...  10 us
    ppermute x1, starting transfers between devices, shards(): lax.ppermute(to_second, ('ta', 'sa'), along_t(others, 1) + along_z(middle))  9.82 us
    all_to_all x1, blocking collectives, sum_over_blocks(): lax.all_to_all(jnp.broadcast_to(s[None], (4,) + s.shape), 'sa', 0, 0, axi...  7.23 us
    ppermute x1, waiting for transfers between devices, sum_over_blocks(): other = lax.ppermute(s, 'sa', pairs)  5.14 us
    ppermute x1, starting transfers between devices, shards(): lax.ppermute(to_first, ('ta', 'sa'), along_z(early) + along_t(late, 0))  4.51 us
    all_gather x1, blocking collectives, gathered_sum(): both = lax.all_gather(x, 'sa', axis_index_groups=groups).astype(F32)  3.36 us
    ppermute x1, starting transfers between devices, sum_over_blocks(): other = lax.ppermute(s, 'sa', pairs)  3.22 us
    all_gather x1, blocking collectives, sum_over_blocks(): other = lax.all_gather(other, 'sa', axis_index_groups=cores)  2.47 us
  transfers between devices with their start and end apart: 4, of which 1 were waited for; matrix products, arithmetic and copies ran while one was open for 0% of the time, Pallas kernels for 3%

profile of v4, /device:TPU:1, one launch (start us, length us, event | category | flops | bytes accessed | tf_op | source)
XLA Modules:
  0.0 52.6 jit_solution(12366408949952171496)
XLA Ops:
  0.6 1.0 %pad_maximum_fusion.packed = bf16[840,128]{1,0:T(8,128)(2,1)S(1)} fusion(bf16[72,128]{1,0:T(8,128)(2,1)} %bitcast.42, bf16[768,128]{1,0:T(8,128)(2,1)} %bitcast.41), kind=kLoop, calls=%fused_computation | loop fusion | flops 430080 | bytes 430080 | tf_op jit(solution)/shard_map/concatenate | solution.py:338
  1.6 0.3 shard_map.59
  1.9 4.5 %collective-permute-start = (bf16[2,3,2,32,128]{4,3,2,1,0:T(8,128)(2,1)S(1)}, bf16[2,3,2,32,128]{4,3,2,1,0:T(8,128)(2,1)S(1)}, u32[]{:S(2)}, u32[]{:S(2)}) collective-permute-start(bf16[2,3,2,32,128]{4,3,2,1,0:T(8,128)(2,1)S(1)} %get-tuple-element.11), channel_id=1, source_target_pairs={{0,23},{1,2},{2,1},{3,4},{4,3},{5,6},{6,5},{7,8},{8,7},{9,10},{10,... | collective-permute-start | bytes 294920 | tf_op jit(solution)/shard_map/ppermute | solution.py:357
  6.4 9.8 %collective-permute-start.1 = (bf16[2,3,2,32,128]{4,3,2,1,0:T(8,128)(2,1)S(1)}, bf16[2,3,2,32,128]{4,3,2,1,0:T(8,128)(2,1)S(1)}, u32[]{:S(2)}, u32[]{:S(2)}) collective-permute-start(bf16[2,3,2,32,128]{4,3,2,1,0:T(8,128)(2,1)S(1)} %get-tuple-element.12), channel_id=1, source_target_pairs={{0,744},{1,745},{2,746},{3,747},{4,748},{5,749},{6,750},{7,751},{8... | collective-permute-start | bytes 294920 | tf_op jit(solution)/shard_map/ppermute | solution.py:358
  16.2 1.9 %collective-permute-start.2 = (bf16[2,3,2,32,128]{4,3,2,1,0:T(8,128)(2,1)S(1)}, bf16[2,3,2,32,128]{4,3,2,1,0:T(8,128)(2,1)S(1)}, u32[]{:S(2)}, u32[]{:S(2)}) collective-permute-start(bf16[2,3,2,32,128]{4,3,2,1,0:T(8,128)(2,1)S(1)} %get-tuple-element.13), channel_id=1, source_target_pairs={{0,24},{1,25},{2,26},{3,27},{4,28},{5,29},{6,30},{7,31},{8,32},{9,... | collective-permute-start | bytes 294920 | tf_op jit(solution)/shard_map/ppermute | solution.py:359
  18.1 0.0 copy-start.1
  18.2 10.0 %all-gather = bf16[4,3,2,32,128]{4,3,2,1,0:T(8,128)(2,1)S(1)} all-gather(bf16[2,3,2,32,128]{4,3,2,1,0:T(8,128)(2,1)S(1)} %get-tuple-element.10), channel_id=2, replica_groups={{0,1},{2,3},{4,5},{6,7},{8,9},{10,11},{12,13},{14,15},{16,17},{18,19},{..., dimensions={0}, use_global_device_ids=true | all-gather | bytes 294912 | tf_op jit(solution)/shard_map/all_gather | solution.py:360
  28.2 0.0 collective-permute-done.first
  28.2 0.0 collective-permute-done.1.second
  28.2 0.0 copy-done.1
  28.2 0.0 copy-start
  28.2 1.1 %shard_map.60.local = f32[2,3,4,32,128]{4,3,2,1,0:T(8,128)S(1)} custom-call(bf16[840,128]{1,0:T(8,128)(2,1)S(1)} %pad_maximum_fusion.packed, bf16[2,3,3,2,128]{4,3,2,1,0:T(2,128)(2,1)S(1)} %bitcast.39, bf16[2,2,3,2,32,128]{5,4,3,2,1,0:T(8,128)(2,1)S(1)} %bitcast.37, bf16[2,3,2,32,128]{4,3,2,1,0:T(8,128)(2,1)S(1)} %collective-permute-done.first, ...), custom_call_target="tpu_custom_call" | custom-call | flops 10240000 | bytes 1010688 | tf_op jit(solution)/shard_map/pallas_call | solution.py:282
  29.3 0.0 collective-permute-done.2.third
  29.3 0.0 copy-done
  29.3 0.4 shard_map.61
  29.7 3.4 %all-gather.1 = f32[4,64,128]{2,1,0:T(8,128)S(1)} all-gather(f32[2,64,128]{2,1,0:T(8,128)S(1)} %get-tuple-element.14), channel_id=3, replica_groups={{0,1},{2,3},{4,5},{6,7},{8,9},{10,11},{12,13},{14,15},{16,17},{18,19},{..., dimensions={0}, use_global_device_ids=true | all-gather | bytes 196608 | tf_op jit(solution)/shard_map/all_gather | solution.py:294
  33.0 3.2 %collective-permute-start.3 = (bf16[2,64,128]{2,1,0:T(8,128)(2,1)S(1)}, bf16[2,64,128]{2,1,0:T(8,128)(2,1)S(1)}, u32[]{:S(2)}, u32[]{:S(2)}) collective-permute-start(bf16[2,64,128]{2,1,0:T(8,128)(2,1)S(1)} %fusion.7), channel_id=1, source_target_pairs={{0,16},{1,9},{2,18},{3,11},{4,20},{5,13},{6,22},{7,15},{8,0},{9,17... | collective-permute-start | bytes 98312 | tf_op jit(solution)/shard_map/ppermute | solution.py:313
  36.3 0.7 %shard_map.62 = bf16[2,3,4,32,128]{4,3,2,1,0:T(8,128)(2,1)} custom-call(bf16[2,3,4,32,128]{4,3,2,1,0:T(8,128)(2,1)S(1)} %get-tuple-element.15.src), custom_call_target="tpu_custom_call" | custom-call | flops 98304 | bytes 393216 | tf_op jit(solution)/shard_map/pallas_call | solution.py:282
  37.0 5.1 %collective-permute-done.3 = bf16[2,64,128]{2,1,0:T(8,128)(2,1)S(1)} collective-permute-done((bf16[2,64,128]{2,1,0:T(8,128)(2,1)S(1)}, bf16[2,64,128]{2,1,0:T(8,128)(2,1)S(1)}, u32[]{:S(2)}, u32[]{:S(2)}) %collective-permute-start.3) | collective-permute-done | bytes 32800 | tf_op jit(solution)/shard_map/ppermute | solution.py:313
  42.1 2.5 %all-gather.2 = bf16[4,64,128]{2,1,0:T(8,128)(2,1)S(1)} all-gather(bf16[2,64,128]{2,1,0:T(8,128)(2,1)S(1)} %collective-permute-done.3), channel_id=4, replica_groups={{0,1},{2,3},{4,5},{6,7},{8,9},{10,11},{12,13},{14,15},{16,17},{18,19},{..., dimensions={0}, use_global_device_ids=true | all-gather | bytes 98304 | tf_op jit(solution)/shard_map/all_gather | solution.py:316
  44.7 7.2 %all_to_all.5 = bf16[4,2,64,128]{3,2,1,0:T(8,128)(2,1)S(1)} all-to-all(bf16[4,2,64,128]{3,2,1,0:T(8,128)(2,1)S(1)} %broadcast_in_dim.10), channel_id=1, replica_groups={{0,2,4,6},{1,3,5,7},{8,10,12,14},{9,11,13,15},{16,18,20,22},{17,19,21,2..., dimensions={0} | all-to-all | bytes 262144 | tf_op jit(solution)/shard_map/all_to_all | solution.py:323
  51.9 0.6 %fusion.5 = f32[2,1,64,128]{3,2,1,0:T(8,128)} fusion(f32[4,2,64,128]{3,2,1,0:T(8,128)S(1)} %convert_element_type.32), kind=kLoop, calls=%fused_computation.13 | loop fusion | flops 49152 | bytes 327680 | tf_op jit(solution)/shard_map/add | solution.py:324
  (4 shorter events, 0.1 us)
Async XLA Ops:
  1.9 26.3 %collective-permute-start = (bf16[2,3,2,32,128]{4,3,2,1,0:T(8,128)(2,1)S(1)}, bf16[2,3,2,32,128]{4,3,2,1,0:T(8,128)(2,1)S(1)}, u32[]{:S(2)}, u32[]{:S(2)}) collective-permute-start(bf16[2,3,2,32,128]{4,3,2,1,0:T(8,128)(2,1)S(1)} %get-tuple-element.11), channel_id=1, source_target_pairs={{0,23},{1,2},{2,1},{3,4},{4,3},{5,6},{6,5},{7,8},{8,7},{9,10},{10,... | collective-permute-start | bytes 294920 | tf_op jit(solution)/shard_map/ppermute | solution.py:357
  6.4 21.8 %collective-permute-start.1 = (bf16[2,3,2,32,128]{4,3,2,1,0:T(8,128)(2,1)S(1)}, bf16[2,3,2,32,128]{4,3,2,1,0:T(8,128)(2,1)S(1)}, u32[]{:S(2)}, u32[]{:S(2)}) collective-permute-start(bf16[2,3,2,32,128]{4,3,2,1,0:T(8,128)(2,1)S(1)} %get-tuple-element.12), channel_id=1, source_target_pairs={{0,744},{1,745},{2,746},{3,747},{4,748},{5,749},{6,750},{7,751},{8... | collective-permute-start | bytes 294920 | tf_op jit(solution)/shard_map/ppermute | solution.py:358
  16.2 13.0 %collective-permute-start.2 = (bf16[2,3,2,32,128]{4,3,2,1,0:T(8,128)(2,1)S(1)}, bf16[2,3,2,32,128]{4,3,2,1,0:T(8,128)(2,1)S(1)}, u32[]{:S(2)}, u32[]{:S(2)}) collective-permute-start(bf16[2,3,2,32,128]{4,3,2,1,0:T(8,128)(2,1)S(1)} %get-tuple-element.13), channel_id=1, source_target_pairs={{0,24},{1,25},{2,26},{3,27},{4,28},{5,29},{6,30},{7,31},{8,32},{9,... | collective-permute-start | bytes 294920 | tf_op jit(solution)/shard_map/ppermute | solution.py:359
  18.1 10.0 %copy-start.1 = (bf16[2,2,3,3,1,1,128]{6,1,5,4,3,2,0:T(2,128)(2,1)S(1)}, bf16[2,2,3,3,1,1,128]{6,1,5,4,3,2,0:T(2,128)(2,1)}, u32[]{:S(2)}) copy-start(bf16[2,2,3,3,1,1,128]{6,1,5,4,3,2,0:T(2,128)(2,1)} %param.6) | copy-start | bytes 27652
  28.2 1.1 %copy-start = (bf16[2,3,64,1,1,128]{5,2,4,3,1,0:T(8,128)(2,1)S(1)}, bf16[2,3,64,1,1,128]{5,2,4,3,1,0:T(8,128)(2,1)}, u32[]{:S(2)}) copy-start(bf16[2,3,64,1,1,128]{5,2,4,3,1,0:T(8,128)(2,1)} %param.7) | copy-start | bytes 294916
  33.0 9.1 %collective-permute-start.3 = (bf16[2,64,128]{2,1,0:T(8,128)(2,1)S(1)}, bf16[2,64,128]{2,1,0:T(8,128)(2,1)S(1)}, u32[]{:S(2)}, u32[]{:S(2)}) collective-permute-start(bf16[2,64,128]{2,1,0:T(8,128)(2,1)S(1)} %fusion.7), channel_id=1, source_target_pairs={{0,16},{1,9},{2,18},{3,11},{4,20},{5,13},{6,22},{7,15},{8,0},{9,17... | collective-permute-start | bytes 98312 | tf_op jit(solution)/shard_map/ppermute | solution.py:313

commit v5 on v3

--- a/solution.py
+++ b/solution.py
@@ -114,14 +114,20 @@
     return out
 
 
-def edge_kernel(ta_size, packed, to_core, to_first, to_second, to_third):
+def knot(ta_size, sa_size):
+    me, z = lax.axis_index("ta"), lax.axis_index("sa")
+    far = (z == 2 * sa_size // 3 - 1) | (z == 2 * sa_size // 3)
+    return far & (me >= ta_size - 2), far & (me == ta_size - 1)
+
+
+def edge_kernel(sizes, packed, to_core, to_zeroth, to_first, to_second, to_third):
     src = Field(packed)
     columns = src.shape[3]
     link_z, link_t = load_links(packed, 2, 3)
     me = lax.axis_index("ta")
     even_z = lax.axis_index("sa") % 2 == 0
     even_t = me % 2 == 0
-    last = me >= ta_size - 2
+    late, last = knot(*sizes)
     for at in range(0, columns, ROWS):
         rows = pl.ds(at, ROWS)
         field = load_field(src, rows, 4)
@@ -136,7 +142,8 @@
                     chip = jnp.where(even_z, minus_z[a][s][q], back_z[q])
                     even = jnp.where(even_t, back_t[q], minus_t[a][s][q])
                     odd = jnp.where(even_t, minus_t[a][s][q], back_t[q])
-                    to_first[q, a, s, rows, :] = jnp.where(last, even, chip).astype(BF16)
+                    to_zeroth[q, a, s, rows, :] = jnp.where(late, even, odd).astype(BF16)
+                    to_first[q, a, s, rows, :] = chip.astype(BF16)
                     to_second[q, a, s, rows, :] = odd.astype(BF16)
                     to_third[q, a, s, rows, :] = jnp.where(last, chip, even).astype(BF16)
 
@@ -159,7 +166,7 @@
     me, core = lax.axis_index("ta"), lax.axis_index("sa") % 2
     ahead_sign = jnp.where(me == ta_size - 1, -1.0, 1.0).astype(F32)
     behind_sign = jnp.where(me == 0, -1.0, 1.0).astype(F32)
-    return core, me % 2, me >= ta_size - 2, ahead_sign, behind_sign
+    return core, me % 2, ahead_sign, behind_sign
 
 
 def chosen_matrix(first, a, b):
@@ -193,13 +200,13 @@
     ]
 
 
-def local_kernel(ta_size, packed, clover, cores, first, second, out):
+def local_kernel(sizes, packed, clover, cores, zeroth, first, second, out):
     src = Field(packed)
     columns = src.shape[3]
-    core, odd_t, last, ahead_sign, behind_sign = place_on_mesh(ta_size)
+    core, odd_t, ahead_sign, behind_sign = place_on_mesh(sizes[0])
+    late, _ = knot(*sizes)
     link = load_links(packed, 0, 1, 2, 3)
-    link_first = chosen_matrix(last, link[3], link[2])
-    forward_first = jnp.where(last, 1 - odd_t, core) == 1
+    forward_zeroth = jnp.where(late, 1 - odd_t, odd_t) == 1
     clov = [load_matrix(clover, 0), load_matrix(clover, 1)]
     for at in range(0, columns, ROWS):
         rows = pl.ds(at, ROWS)
@@ -224,8 +231,9 @@
                 upper = [add(w[s], g[s]) for s in range(2)]
                 add_to(hop, a, upper + spin_dagger(direction, [sub(g[s], w[s]) for s in range(2)]))
         add_swapped(hop, link[2], load_field(cores.at[1 - core], rows, 2), core == 0, turned_z)
-        add_swapped(hop, link_first, load_field(first, rows, 2), forward_first, functools.partial(turned_either, last))
+        add_swapped(hop, link[2], load_field(first, rows, 2), core == 1, turned_z)
         add_swapped(hop, link[3], load_field(second, rows, 2), odd_t == 1, turned_t, ahead_sign, behind_sign)
+        add_swapped(hop, link[3], load_field(zeroth, rows, 2), forward_zeroth, turned_t, ahead_sign, behind_sign)
         for a in range(3):
             for s in range(4):
                 own = add(field[a][s], color_row(clov[s // 2], field, a, s, False))
@@ -233,9 +241,10 @@
                     out[q, a, s, rows, :] = own[q] - KAPPA * hop[a][s][q]
 
 
-def finish_kernel(ta_size, local, packed, third, vectors, result, partial):
+def finish_kernel(sizes, local, packed, third, vectors, result, partial):
     columns = local.shape[3]
-    core, odd_t, last, _, _ = place_on_mesh(ta_size)
+    core, odd_t, _, _ = place_on_mesh(sizes[0])
+    _, last = knot(*sizes)
     link = chosen_matrix(last, *load_links(packed, 2, 3))
     forward = jnp.where(last, core, 1 - odd_t) == 1
     turn = functools.partial(turned_either, jnp.logical_not(last))
@@ -284,7 +293,7 @@
     return lax.reduce_precision(both[0] + both[1], 8, 7).astype(BF16)
 
 
-def sum_over_blocks(partial, size):
+def sum_over_blocks(partial, result, size):
     plane = 8
     planes = size // plane
     cores = [[i, i + 1] for i in range(0, size, 2)]
@@ -292,22 +301,25 @@
     even = [[z + 4 * p + c, z + 4 * p + 2 + c] for z in starts for p in range(2) for c in range(2)]
     odd = [[z + 2 + c, z + 4 + c] for z in starts for c in range(2)]
     odd += [[z + c, z + 6 + c] for z in starts for c in range(2)]
+    row = [[z + 2 * x + c for x in range(4)] for z in starts for c in range(2)]
     s = gathered_sum(partial, cores)
-    row = [[z + 2 * x + c for x in range(4)] for z in starts for c in range(2)]
-    four = lax.all_to_all(jnp.broadcast_to(s[None], (4,) + s.shape), "sa", 0, 0, axis_index_groups=row).astype(F32)
-    s = lax.reduce_precision((four[0] + four[1]) + (four[2] + four[3]), 8, 7).astype(BF16)
     pairs = []
     for i in range(size):
         z, r = divmod(i, plane)
         step = 1 if i % 2 else planes - 1
         pairs.append((i, ((z + step) % planes) * plane + r))
-    other = lax.all_gather(lax.ppermute(s, "sa", pairs), "sa", axis_index_groups=cores)
+    other = lax.ppermute(s, "sa", pairs)
+    (result,) = call(copy_kernel, [jax.ShapeDtypeStruct(result.shape, BF16)], (result,), result.size)
+    other, result = lax.optimization_barrier((other, result))
+    other = lax.all_gather(other, "sa", axis_index_groups=cores)
     z = lax.axis_index("sa") // plane
     own, nxt, last = s.astype(F32), other[0].astype(F32), other[1].astype(F32)
     first = jnp.where(z == 0, own, jnp.where(z == 1, last, nxt))
     second = jnp.where(z == 0, nxt, jnp.where(z == 1, own, last))
     third = jnp.where(z == 0, last, jnp.where(z == 1, nxt, own))
-    return first + second + third
+    s = lax.reduce_precision(first + second + third, 8, 7).astype(BF16)
+    four = lax.all_to_all(jnp.broadcast_to(s[None], (4,) + s.shape), "sa", 0, 0, axis_index_groups=row).astype(F32)
+    return (four[0] + four[1]) + (four[2] + four[3]), result
 
 
 def shards(source_field, gauge_links, clover, eigenvectors):
@@ -322,9 +334,9 @@
     points = columns * sites
 
     packed = jnp.concatenate([src.reshape(-1, sites), links.reshape(-1, sites)])
-    to_core, to_first, to_second, to_third = call(
-        functools.partial(edge_kernel, ta),
-        [half_shape] * 4,
+    to_core, to_zeroth, to_first, to_second, to_third = call(
+        functools.partial(edge_kernel, (ta, sa)),
+        [half_shape] * 5,
         (packed,),
         500 * points,
     )
@@ -332,25 +344,32 @@
     def place(t, z):
         return (t % ta) * sa + z % sa
 
-    def along_z(slabs):
-        return [(place(t, z), place(t, z + (1 if z % 2 else -1))) for t in slabs for z in range(sa)]
-
-    def along_t(slabs, parity):
-        return [(place(t, z), place(t + (1 if t % 2 == parity else -1), z)) for t in slabs for z in range(sa)]
-
-    most, rest = range(ta - 2), range(ta - 2, ta)
-    first = lax.ppermute(to_first, ("ta", "sa"), along_z(most) + along_t(rest, 0))
-    second = lax.ppermute(to_second, ("ta", "sa"), along_t(range(ta), 1))
-    third = lax.ppermute(to_third, ("ta", "sa"), along_t(most, 0) + along_z(rest))
+    def along_z(slabs, blocks):
+        return [(place(t, z), place(t, z + (1 if z % 2 else -1))) for t in slabs for z in blocks]
+
+    def along_t(slabs, parity, blocks):
+        return [(place(t, z), place(t + (1 if t % 2 == parity else -1), z)) for t in slabs for z in blocks]
+
+    slabs, late, last = range(ta), (ta - 2, ta - 1), (ta - 1,)
+    waiting = (0, sa // 3 - 1)
+    far = (2 * sa // 3 - 1, 2 * sa // 3)
+    rest = [z for z in range(sa) if z not in waiting]
+    near = [z for z in range(sa) if z not in far]
+    zeroth = lax.ppermute(to_zeroth, ("ta", "sa"), along_t(slabs, 1, waiting) + along_t(late, 0, far))
+    first = lax.ppermute(to_first, ("ta", "sa"), along_z(slabs[:-1], range(sa)) + along_z(last, near))
+    second = lax.ppermute(to_second, ("ta", "sa"), along_t(slabs, 1, rest))
+    third = lax.ppermute(
+        to_third, ("ta", "sa"), along_t(slabs[:-2], 0, range(sa)) + along_t(late, 0, near) + along_z(last, far)
+    )
     cores = lax.all_gather(to_core, "sa", axis_index_groups=[[i, i + 1] for i in range(0, sa, 2)])
     (local,) = call(
-        functools.partial(local_kernel, ta),
+        functools.partial(local_kernel, (ta, sa)),
         [jax.ShapeDtypeStruct((2, 3, 4, columns, sites), F32)],
-        (packed, clov, cores, first, second),
+        (packed, clov, cores, zeroth, first, second),
         2500 * points,
     )
     result, partial = call(
-        functools.partial(finish_kernel, ta),
+        functools.partial(finish_kernel, (ta, sa)),
         [
             jax.ShapeDtypeStruct((2, 3, 4, columns, sites), BF16),
             jax.ShapeDtypeStruct((2, vectors.shape[2], 4 * columns), F32),
@@ -358,8 +377,7 @@
         (local, packed, third, vectors),
         500 * points,
     )
-    perambulator = sum_over_blocks(partial, sa)
-    (result,) = call(copy_kernel, [jax.ShapeDtypeStruct(result.shape, BF16)], (result,), 2000 * points)
+    perambulator, result = sum_over_blocks(partial, result, sa)
     return result.reshape(source_field.shape), perambulator[:, None]
 
 

time: 54.2 us -> 51.7 us (0.954)
  blocking collectives: 24.7 us -> 18.2 us
  starting transfers between devices: 20.9 us -> 26.6 us
  waiting for transfers between devices: 3.18 us -> 1.37 us
    ppermute x4 -> x5, starting transfers between devices: 20.9 us -> 26.6 us  [the longest x1 10.5 us: shards(): second = lax.ppermute(to_second, ('ta', 'sa'), along_t(slabs, 1, rest))]
    all_gather x1, blocking collectives: 10 us -> 6.48 us  [shards(): lax.all_gather(to_core, 'sa', axis_index_groups=[[i, i + 1] for i in rang...]
    all_gather x1, blocking collectives: 4.13 us -> 2.12 us  [sum_over_blocks(): other = lax.all_gather(other, 'sa', axis_index_groups=cores)]
    ppermute x4 -> x5, waiting for transfers between devices: 3.18 us -> 1.37 us  [the longest x1 1.36 us: sum_over_blocks(): other = lax.ppermute(s, 'sa', pairs)]
    all_gather x1, blocking collectives: 3.35 us -> 1.91 us  [gathered_sum(): both = lax.all_gather(x, 'sa', axis_index_groups=groups).astype(F32)]
    unnamed x1 -> x0, other arithmetic: 0.67 us -> none
    add x0 -> x1, other arithmetic: none -> 0.65 us  [sum_over_blocks(): return (four[0] + four[1] + (four[2] + four[3]), result)]
  transfers between devices with their start and end apart: 4 -> 5, of which waited for: 1 -> 1; matrix products, arithmetic and copies ran while one was open for 0% -> 0% of each run, Pallas kernels for 3% -> 4%
where the time goes in v5:
time: 51.7 us; the launch traced here: 51.2 us
  starting transfers between devices  26.6 us (51%)
  blocking collectives  18.2 us (35%)
  Pallas kernels  2.49 us (5%)
  other arithmetic  1.67 us (3%)
  waiting for transfers between devices  1.37 us (3%)
  between operations  0.79 us (2%)
    ppermute x1, starting transfers between devices, shards(): second = lax.ppermute(to_second, ('ta', 'sa'), along_t(slabs, 1, rest))  10.5 us
    ppermute x1, starting transfers between devices, sum_over_blocks(): other = lax.ppermute(s, 'sa', pairs)  9.02 us
    all_to_all x1, blocking collectives, sum_over_blocks(): lax.all_to_all(jnp.broadcast_to(s[None], (4,) + s.shape), 'sa', 0, 0, axi...  7.65 us
    all_gather x1, blocking collectives, shards(): lax.all_gather(to_core, 'sa', axis_index_groups=[[i, i + 1] for i in rang...  6.48 us
    ppermute x1, starting transfers between devices, shards(): lax.ppermute(to_first, ('ta', 'sa'), along_z(slabs[:-1], range(sa)) + alo...  4.51 us
    pallas_call x4, Pallas kernels, call(): pl.pallas_call(body, out_shape=outs, in_specs=in_specs or [vmem] * len(op...  2.49 us
    all_gather x1, blocking collectives, sum_over_blocks(): other = lax.all_gather(other, 'sa', axis_index_groups=cores)  2.12 us
    ppermute x1, starting transfers between devices, shards(): lax.ppermute(to_third, ('ta', 'sa'), along_t(slabs[:-2], 0, range(sa)) +...  1.92 us
  transfers between devices with their start and end apart: 5, of which 1 were waited for; matrix products, arithmetic and copies ran while one was open for 0% of the time, Pallas kernels for 4%

profile of v5, /device:TPU:1, one launch (start us, length us, event | category | flops | bytes accessed | tf_op | source)
XLA Modules:
  0.0 51.2 jit_solution(15225816512857265887)
XLA Ops:
  0.6 1.0 %pad_maximum_fusion.packed = bf16[840,128]{1,0:T(8,128)(2,1)S(1)} fusion(bf16[72,128]{1,0:T(8,128)(2,1)} %bitcast.42, bf16[768,128]{1,0:T(8,128)(2,1)} %bitcast.41), kind=kLoop, calls=%fused_computation | loop fusion | flops 430080 | bytes 430080 | tf_op jit(solution)/shard_map/concatenate | solution.py:336
  1.6 0.3 shard_map.59
  1.9 0.7 %collective-permute-start = (bf16[2,3,2,32,128]{4,3,2,1,0:T(8,128)(2,1)S(1)}, bf16[2,3,2,32,128]{4,3,2,1,0:T(8,128)(2,1)S(1)}, u32[]{:S(2)}, u32[]{:S(2)}) collective-permute-start(bf16[2,3,2,32,128]{4,3,2,1,0:T(8,128)(2,1)S(1)} %get-tuple-element.12), channel_id=1, source_target_pairs={{0,744},{7,751},{24,48},{31,55},{48,24},{55,31},{72,96},{79,103},{... | collective-permute-start | bytes 294920 | tf_op jit(solution)/shard_map/ppermute | solution.py:358
  2.5 4.5 %collective-permute-start.1 = (bf16[2,3,2,32,128]{4,3,2,1,0:T(8,128)(2,1)S(1)}, bf16[2,3,2,32,128]{4,3,2,1,0:T(8,128)(2,1)S(1)}, u32[]{:S(2)}, u32[]{:S(2)}) collective-permute-start(bf16[2,3,2,32,128]{4,3,2,1,0:T(8,128)(2,1)S(1)} %get-tuple-element.13), channel_id=1, source_target_pairs={{0,23},{1,2},{2,1},{3,4},{4,3},{5,6},{6,5},{7,8},{8,7},{9,10},{10,... | collective-permute-start | bytes 294920 | tf_op jit(solution)/shard_map/ppermute | solution.py:359
  7.1 10.5 %collective-permute-start.2 = (bf16[2,3,2,32,128]{4,3,2,1,0:T(8,128)(2,1)S(1)}, bf16[2,3,2,32,128]{4,3,2,1,0:T(8,128)(2,1)S(1)}, u32[]{:S(2)}, u32[]{:S(2)}) collective-permute-start(bf16[2,3,2,32,128]{4,3,2,1,0:T(8,128)(2,1)S(1)} %get-tuple-element.14), channel_id=1, source_target_pairs={{1,745},{2,746},{3,747},{4,748},{5,749},{6,750},{8,752},{9,753},{1... | collective-permute-start | bytes 294920 | tf_op jit(solution)/shard_map/ppermute | solution.py:360
  17.6 1.9 %collective-permute-start.3 = (bf16[2,3,2,32,128]{4,3,2,1,0:T(8,128)(2,1)S(1)}, bf16[2,3,2,32,128]{4,3,2,1,0:T(8,128)(2,1)S(1)}, u32[]{:S(2)}, u32[]{:S(2)}) collective-permute-start(bf16[2,3,2,32,128]{4,3,2,1,0:T(8,128)(2,1)S(1)} %get-tuple-element.15), channel_id=1, source_target_pairs={{0,24},{1,25},{2,26},{3,27},{4,28},{5,29},{6,30},{7,31},{8,32},{9,... | collective-permute-start | bytes 294920 | tf_op jit(solution)/shard_map/ppermute | solution.py:361
  19.5 0.0 copy-start.1
  19.5 6.5 %all-gather = bf16[4,3,2,32,128]{4,3,2,1,0:T(8,128)(2,1)S(1)} all-gather(bf16[2,3,2,32,128]{4,3,2,1,0:T(8,128)(2,1)S(1)} %get-tuple-element.11), channel_id=2, replica_groups={{0,1},{2,3},{4,5},{6,7},{8,9},{10,11},{12,13},{14,15},{16,17},{18,19},{..., dimensions={0}, use_global_device_ids=true | all-gather | bytes 294912 | tf_op jit(solution)/shard_map/all_gather | solution.py:364
  26.0 0.0 collective-permute-done.zeroth
  26.0 0.0 collective-permute-done.1.first
  26.0 0.0 collective-permute-done.2.second
  26.0 0.0 copy-done.1
  26.0 0.0 copy-start
  26.0 1.2 %shard_map.60.local = f32[2,3,4,32,128]{4,3,2,1,0:T(8,128)S(1)} custom-call(bf16[840,128]{1,0:T(8,128)(2,1)S(1)} %pad_maximum_fusion.packed, bf16[2,3,3,2,128]{4,3,2,1,0:T(2,128)(2,1)S(1)} %bitcast.39, bf16[2,2,3,2,32,128]{5,4,3,2,1,0:T(8,128)(2,1)S(1)} %bitcast.37, bf16[2,3,2,32,128]{4,3,2,1,0:T(8,128)(2,1)S(1)} %collective-permute-done.zeroth, ...), custom_call_target="tpu_custom_call" | custom-call | flops 10240000 | bytes 1108992 | tf_op jit(solution)/shard_map/pallas_call | solution.py:280
  27.2 0.0 collective-permute-done.3.third
  27.2 0.0 copy-done
  27.2 0.4 shard_map.61
  27.6 1.9 %all-gather.1 = f32[4,64,128]{2,1,0:T(8,128)S(1)} all-gather(f32[2,64,128]{2,1,0:T(8,128)S(1)} %get-tuple-element.16), channel_id=3, replica_groups={{0,1},{2,3},{4,5},{6,7},{8,9},{10,11},{12,13},{14,15},{16,17},{18,19},{..., dimensions={0}, use_global_device_ids=true | all-gather | bytes 196608 | tf_op jit(solution)/shard_map/all_gather | solution.py:292
  29.5 9.0 %collective-permute-start.4 = (bf16[2,64,128]{2,1,0:T(8,128)(2,1)S(1)}, bf16[2,64,128]{2,1,0:T(8,128)(2,1)S(1)}, u32[]{:S(2)}, u32[]{:S(2)}) collective-permute-start(bf16[2,64,128]{2,1,0:T(8,128)(2,1)S(1)} %fusion.7), channel_id=1, source_target_pairs={{0,16},{1,9},{2,18},{3,11},{4,20},{5,13},{6,22},{7,15},{8,0},{9,17... | collective-permute-start | bytes 98312 | tf_op jit(solution)/shard_map/ppermute | solution.py:311
  38.6 0.7 %shard_map.62 = bf16[2,3,4,32,128]{4,3,2,1,0:T(8,128)(2,1)} custom-call(bf16[2,3,4,32,128]{4,3,2,1,0:T(8,128)(2,1)S(1)} %get-tuple-element.17.src), custom_call_target="tpu_custom_call" | custom-call | flops 98304 | bytes 393216 | tf_op jit(solution)/shard_map/pallas_call | solution.py:280
  39.3 1.4 %collective-permute-done.4 = bf16[2,64,128]{2,1,0:T(8,128)(2,1)S(1)} collective-permute-done((bf16[2,64,128]{2,1,0:T(8,128)(2,1)S(1)}, bf16[2,64,128]{2,1,0:T(8,128)(2,1)S(1)}, u32[]{:S(2)}, u32[]{:S(2)}) %collective-permute-start.4) | collective-permute-done | bytes 32800 | tf_op jit(solution)/shard_map/ppermute | solution.py:311
  40.6 2.1 %all-gather.2 = bf16[4,64,128]{2,1,0:T(8,128)(2,1)S(1)} all-gather(bf16[2,64,128]{2,1,0:T(8,128)(2,1)S(1)} %collective-permute-done.4), channel_id=4, replica_groups={{0,1},{2,3},{4,5},{6,7},{8,9},{10,11},{12,13},{14,15},{16,17},{18,19},{..., dimensions={0}, use_global_device_ids=true | all-gather | bytes 98304 | tf_op jit(solution)/shard_map/all_gather | solution.py:314
  42.8 7.6 %all_to_all.5 = bf16[4,2,64,128]{3,2,1,0:T(8,128)(2,1)S(1)} all-to-all(bf16[4,2,64,128]{3,2,1,0:T(8,128)(2,1)S(1)} %broadcast_in_dim.10), channel_id=1, replica_groups={{0,2,4,6},{1,3,5,7},{8,10,12,14},{9,11,13,15},{16,18,20,22},{17,19,21,2..., dimensions={0} | all-to-all | bytes 262144 | tf_op jit(solution)/shard_map/all_to_all | solution.py:321
  50.5 0.6 %fusion.5 = f32[2,1,64,128]{3,2,1,0:T(8,128)} fusion(f32[4,2,64,128]{3,2,1,0:T(8,128)S(1)} %convert_element_type.32), kind=kLoop, calls=%fused_computation.13 | loop fusion | flops 49152 | bytes 327680 | tf_op jit(solution)/shard_map/add | solution.py:322
  (4 shorter events, 0.1 us)
Async XLA Ops:
  1.9 24.1 %collective-permute-start = (bf16[2,3,2,32,128]{4,3,2,1,0:T(8,128)(2,1)S(1)}, bf16[2,3,2,32,128]{4,3,2,1,0:T(8,128)(2,1)S(1)}, u32[]{:S(2)}, u32[]{:S(2)}) collective-permute-start(bf16[2,3,2,32,128]{4,3,2,1,0:T(8,128)(2,1)S(1)} %get-tuple-element.12), channel_id=1, source_target_pairs={{0,744},{7,751},{24,48},{31,55},{48,24},{55,31},{72,96},{79,103},{... | collective-permute-start | bytes 294920 | tf_op jit(solution)/shard_map/ppermute | solution.py:358
  2.5 23.5 %collective-permute-start.1 = (bf16[2,3,2,32,128]{4,3,2,1,0:T(8,128)(2,1)S(1)}, bf16[2,3,2,32,128]{4,3,2,1,0:T(8,128)(2,1)S(1)}, u32[]{:S(2)}, u32[]{:S(2)}) collective-permute-start(bf16[2,3,2,32,128]{4,3,2,1,0:T(8,128)(2,1)S(1)} %get-tuple-element.13), channel_id=1, source_target_pairs={{0,23},{1,2},{2,1},{3,4},{4,3},{5,6},{6,5},{7,8},{8,7},{9,10},{10,... | collective-permute-start | bytes 294920 | tf_op jit(solution)/shard_map/ppermute | solution.py:359
  7.1 19.0 %collective-permute-start.2 = (bf16[2,3,2,32,128]{4,3,2,1,0:T(8,128)(2,1)S(1)}, bf16[2,3,2,32,128]{4,3,2,1,0:T(8,128)(2,1)S(1)}, u32[]{:S(2)}, u32[]{:S(2)}) collective-permute-start(bf16[2,3,2,32,128]{4,3,2,1,0:T(8,128)(2,1)S(1)} %get-tuple-element.14), channel_id=1, source_target_pairs={{1,745},{2,746},{3,747},{4,748},{5,749},{6,750},{8,752},{9,753},{1... | collective-permute-start | bytes 294920 | tf_op jit(solution)/shard_map/ppermute | solution.py:360
  17.6 9.6 %collective-permute-start.3 = (bf16[2,3,2,32,128]{4,3,2,1,0:T(8,128)(2,1)S(1)}, bf16[2,3,2,32,128]{4,3,2,1,0:T(8,128)(2,1)S(1)}, u32[]{:S(2)}, u32[]{:S(2)}) collective-permute-start(bf16[2,3,2,32,128]{4,3,2,1,0:T(8,128)(2,1)S(1)} %get-tuple-element.15), channel_id=1, source_target_pairs={{0,24},{1,25},{2,26},{3,27},{4,28},{5,29},{6,30},{7,31},{8,32},{9,... | collective-permute-start | bytes 294920 | tf_op jit(solution)/shard_map/ppermute | solution.py:361
  19.5 6.5 %copy-start.1 = (bf16[2,2,3,3,1,1,128]{6,1,5,4,3,2,0:T(2,128)(2,1)S(1)}, bf16[2,2,3,3,1,1,128]{6,1,5,4,3,2,0:T(2,128)(2,1)}, u32[]{:S(2)}) copy-start(bf16[2,2,3,3,1,1,128]{6,1,5,4,3,2,0:T(2,128)(2,1)} %param.6) | copy-start | bytes 27652
  26.0 1.2 %copy-start = (bf16[2,3,64,1,1,128]{5,2,4,3,1,0:T(8,128)(2,1)S(1)}, bf16[2,3,64,1,1,128]{5,2,4,3,1,0:T(8,128)(2,1)}, u32[]{:S(2)}) copy-start(bf16[2,3,64,1,1,128]{5,2,4,3,1,0:T(8,128)(2,1)} %param.7) | copy-start | bytes 294916
  29.5 11.1 %collective-permute-start.4 = (bf16[2,64,128]{2,1,0:T(8,128)(2,1)S(1)}, bf16[2,64,128]{2,1,0:T(8,128)(2,1)S(1)}, u32[]{:S(2)}, u32[]{:S(2)}) collective-permute-start(bf16[2,64,128]{2,1,0:T(8,128)(2,1)S(1)} %fusion.7), channel_id=1, source_target_pairs={{0,16},{1,9},{2,18},{3,11},{4,20},{5,13},{6,22},{7,15},{8,0},{9,17... | collective-permute-start | bytes 98312 | tf_op jit(solution)/shard_map/ppermute | solution.py:311

commit v6 on v5

--- a/solution.py
+++ b/solution.py
@@ -351,13 +351,14 @@
         return [(place(t, z), place(t + (1 if t % 2 == parity else -1), z)) for t in slabs for z in blocks]
 
     slabs, late, last = range(ta), (ta - 2, ta - 1), (ta - 1,)
+    ends = (0, ta - 1)
     waiting = (0, sa // 3 - 1)
     far = (2 * sa // 3 - 1, 2 * sa // 3)
     rest = [z for z in range(sa) if z not in waiting]
     near = [z for z in range(sa) if z not in far]
-    zeroth = lax.ppermute(to_zeroth, ("ta", "sa"), along_t(slabs, 1, waiting) + along_t(late, 0, far))
+    zeroth = lax.ppermute(to_zeroth, ("ta", "sa"), along_t(slabs[1:-1], 1, waiting) + along_t(ends, 1, waiting[1:]) + along_t(late, 0, far))
     first = lax.ppermute(to_first, ("ta", "sa"), along_z(slabs[:-1], range(sa)) + along_z(last, near))
-    second = lax.ppermute(to_second, ("ta", "sa"), along_t(slabs, 1, rest))
+    second = lax.ppermute(to_second, ("ta", "sa"), along_t(slabs, 1, rest) + along_t(ends, 1, waiting[:1]))
     third = lax.ppermute(
         to_third, ("ta", "sa"), along_t(slabs[:-2], 0, range(sa)) + along_t(late, 0, near) + along_z(last, far)
     )

time: 51.7 us -> 56.7 us (1.097)
  blocking collectives: 18.2 us -> 25.9 us
  starting transfers between devices: 26.6 us -> 19.5 us
  waiting for transfers between devices: 1.37 us -> 5.92 us
    ppermute x1, starting transfers between devices: 9.02 us -> 1.92 us  [sum_over_blocks(): other = lax.ppermute(s, 'sa', pairs)]
    all_gather x1, blocking collectives: 6.48 us -> 12.4 us  [shards(): lax.all_gather(to_core, 'sa', axis_index_groups=[[i, i + 1] for i in rang...]
    ppermute x1, waiting for transfers between devices: 1.36 us -> 5.91 us  [sum_over_blocks(): other = lax.ppermute(s, 'sa', pairs)]
    all_gather x1, blocking collectives: 1.91 us -> 3.31 us  [gathered_sum(): both = lax.all_gather(x, 'sa', axis_index_groups=groups).astype(F32)]
    all_gather x1, blocking collectives: 2.12 us -> 3 us  [sum_over_blocks(): other = lax.all_gather(other, 'sa', axis_index_groups=cores)]
  transfers between devices with their start and end apart: 5 -> 5, of which waited for: 1 -> 1; matrix products, arithmetic and copies ran while one was open for 0% -> 0% of each run, Pallas kernels for 4% -> 3%
where the time goes in v6:
time: 56.7 us; the launch traced here: 56.3 us
  blocking collectives  25.9 us (46%)
  starting transfers between devices  19.5 us (34%)
  waiting for transfers between devices  5.92 us (10%)
  Pallas kernels  2.48 us (4%)
  other arithmetic  1.67 us (3%)
  between operations  0.79 us (1%)
    all_gather x1, blocking collectives, shards(): lax.all_gather(to_core, 'sa', axis_index_groups=[[i, i + 1] for i in rang...  12.4 us
    ppermute x1, starting transfers between devices, shards(): lax.ppermute(to_second, ('ta', 'sa'), along_t(slabs, 1, rest) + along_t(e...  10.5 us
    all_to_all x1, blocking collectives, sum_over_blocks(): lax.all_to_all(jnp.broadcast_to(s[None], (4,) + s.shape), 'sa', 0, 0, axi...  7.23 us
    ppermute x1, waiting for transfers between devices, sum_over_blocks(): other = lax.ppermute(s, 'sa', pairs)  5.91 us
    ppermute x1, starting transfers between devices, shards(): lax.ppermute(to_first, ('ta', 'sa'), along_z(slabs[:-1], range(sa)) + alo...  4.51 us
    all_gather x1, blocking collectives, gathered_sum(): both = lax.all_gather(x, 'sa', axis_index_groups=groups).astype(F32)  3.31 us
    all_gather x1, blocking collectives, sum_over_blocks(): other = lax.all_gather(other, 'sa', axis_index_groups=cores)  3 us
    pallas_call x4, Pallas kernels, call(): pl.pallas_call(body, out_shape=outs, in_specs=in_specs or [vmem] * len(op...  2.48 us
  transfers between devices with their start and end apart: 5, of which 1 were waited for; matrix products, arithmetic and copies ran while one was open for 0% of the time, Pallas kernels for 3%

profile of v6, /device:TPU:1, one launch (start us, length us, event | category | flops | bytes accessed | tf_op | source)
XLA Modules:
  0.0 56.3 jit_solution(9065716851782947968)
XLA Ops:
  0.6 1.0 %pad_maximum_fusion.packed = bf16[840,128]{1,0:T(8,128)(2,1)S(1)} fusion(bf16[72,128]{1,0:T(8,128)(2,1)} %bitcast.42, bf16[768,128]{1,0:T(8,128)(2,1)} %bitcast.41), kind=kLoop, calls=%fused_computation | loop fusion | flops 430080 | bytes 430080 | tf_op jit(solution)/shard_map/concatenate | solution.py:336
  1.6 0.3 shard_map.59
  1.9 0.7 %collective-permute-start = (bf16[2,3,2,32,128]{4,3,2,1,0:T(8,128)(2,1)S(1)}, bf16[2,3,2,32,128]{4,3,2,1,0:T(8,128)(2,1)S(1)}, u32[]{:S(2)}, u32[]{:S(2)}) collective-permute-start(bf16[2,3,2,32,128]{4,3,2,1,0:T(8,128)(2,1)S(1)} %get-tuple-element.12), channel_id=1, source_target_pairs={{24,48},{31,55},{48,24},{55,31},{72,96},{79,103},{96,72},{103,79},... | collective-permute-start | bytes 294920 | tf_op jit(solution)/shard_map/ppermute | solution.py:359
  2.5 4.5 %collective-permute-start.1 = (bf16[2,3,2,32,128]{4,3,2,1,0:T(8,128)(2,1)S(1)}, bf16[2,3,2,32,128]{4,3,2,1,0:T(8,128)(2,1)S(1)}, u32[]{:S(2)}, u32[]{:S(2)}) collective-permute-start(bf16[2,3,2,32,128]{4,3,2,1,0:T(8,128)(2,1)S(1)} %get-tuple-element.13), channel_id=1, source_target_pairs={{0,23},{1,2},{2,1},{3,4},{4,3},{5,6},{6,5},{7,8},{8,7},{9,10},{10,... | collective-permute-start | bytes 294920 | tf_op jit(solution)/shard_map/ppermute | solution.py:360
  7.1 10.5 %collective-permute-start.2 = (bf16[2,3,2,32,128]{4,3,2,1,0:T(8,128)(2,1)S(1)}, bf16[2,3,2,32,128]{4,3,2,1,0:T(8,128)(2,1)S(1)}, u32[]{:S(2)}, u32[]{:S(2)}) collective-permute-start(bf16[2,3,2,32,128]{4,3,2,1,0:T(8,128)(2,1)S(1)} %get-tuple-element.14), channel_id=1, source_target_pairs={{1,745},{2,746},{3,747},{4,748},{5,749},{6,750},{8,752},{9,753},{1... | collective-permute-start | bytes 294920 | tf_op jit(solution)/shard_map/ppermute | solution.py:361
  17.6 1.9 %collective-permute-start.3 = (bf16[2,3,2,32,128]{4,3,2,1,0:T(8,128)(2,1)S(1)}, bf16[2,3,2,32,128]{4,3,2,1,0:T(8,128)(2,1)S(1)}, u32[]{:S(2)}, u32[]{:S(2)}) collective-permute-start(bf16[2,3,2,32,128]{4,3,2,1,0:T(8,128)(2,1)S(1)} %get-tuple-element.15), channel_id=1, source_target_pairs={{0,24},{1,25},{2,26},{3,27},{4,28},{5,29},{6,30},{7,31},{8,32},{9,... | collective-permute-start | bytes 294920 | tf_op jit(solution)/shard_map/ppermute | solution.py:362
  19.5 0.0 copy-start.1
  19.5 12.4 %all-gather = bf16[4,3,2,32,128]{4,3,2,1,0:T(8,128)(2,1)S(1)} all-gather(bf16[2,3,2,32,128]{4,3,2,1,0:T(8,128)(2,1)S(1)} %get-tuple-element.11), channel_id=2, replica_groups={{0,1},{2,3},{4,5},{6,7},{8,9},{10,11},{12,13},{14,15},{16,17},{18,19},{..., dimensions={0}, use_global_device_ids=true | all-gather | bytes 294912 | tf_op jit(solution)/shard_map/all_gather | solution.py:365
  31.9 0.0 collective-permute-done.zeroth
  31.9 0.0 collective-permute-done.1.first
  31.9 0.0 collective-permute-done.2.second
  31.9 0.0 copy-done.1
  31.9 0.0 copy-start
  31.9 1.2 %shard_map.60.local = f32[2,3,4,32,128]{4,3,2,1,0:T(8,128)S(1)} custom-call(bf16[840,128]{1,0:T(8,128)(2,1)S(1)} %pad_maximum_fusion.packed, bf16[2,3,3,2,128]{4,3,2,1,0:T(2,128)(2,1)S(1)} %bitcast.39, bf16[2,2,3,2,32,128]{5,4,3,2,1,0:T(8,128)(2,1)S(1)} %bitcast.37, bf16[2,3,2,32,128]{4,3,2,1,0:T(8,128)(2,1)S(1)} %collective-permute-done.zeroth, ...), custom_call_target="tpu_custom_call" | custom-call | flops 10240000 | bytes 1108992 | tf_op jit(solution)/shard_map/pallas_call | solution.py:280
  33.1 0.0 collective-permute-done.3.third
  33.1 0.0 copy-done
  33.1 0.4 shard_map.61
  33.5 3.3 %all-gather.1 = f32[4,64,128]{2,1,0:T(8,128)S(1)} all-gather(f32[2,64,128]{2,1,0:T(8,128)S(1)} %get-tuple-element.16), channel_id=3, replica_groups={{0,1},{2,3},{4,5},{6,7},{8,9},{10,11},{12,13},{14,15},{16,17},{18,19},{..., dimensions={0}, use_global_device_ids=true | all-gather | bytes 196608 | tf_op jit(solution)/shard_map/all_gather | solution.py:292
  36.8 1.9 %collective-permute-start.4 = (bf16[2,64,128]{2,1,0:T(8,128)(2,1)S(1)}, bf16[2,64,128]{2,1,0:T(8,128)(2,1)S(1)}, u32[]{:S(2)}, u32[]{:S(2)}) collective-permute-start(bf16[2,64,128]{2,1,0:T(8,128)(2,1)S(1)} %fusion.7), channel_id=1, source_target_pairs={{0,16},{1,9},{2,18},{3,11},{4,20},{5,13},{6,22},{7,15},{8,0},{9,17... | collective-permute-start | bytes 98312 | tf_op jit(solution)/shard_map/ppermute | solution.py:311
  38.8 0.7 %shard_map.62 = bf16[2,3,4,32,128]{4,3,2,1,0:T(8,128)(2,1)} custom-call(bf16[2,3,4,32,128]{4,3,2,1,0:T(8,128)(2,1)S(1)} %get-tuple-element.17.src), custom_call_target="tpu_custom_call" | custom-call | flops 98304 | bytes 393216 | tf_op jit(solution)/shard_map/pallas_call | solution.py:280
  39.5 5.9 %collective-permute-done.4 = bf16[2,64,128]{2,1,0:T(8,128)(2,1)S(1)} collective-permute-done((bf16[2,64,128]{2,1,0:T(8,128)(2,1)S(1)}, bf16[2,64,128]{2,1,0:T(8,128)(2,1)S(1)}, u32[]{:S(2)}, u32[]{:S(2)}) %collective-permute-start.4) | collective-permute-done | bytes 32800 | tf_op jit(solution)/shard_map/ppermute | solution.py:311
  45.4 3.0 %all-gather.2 = bf16[4,64,128]{2,1,0:T(8,128)(2,1)S(1)} all-gather(bf16[2,64,128]{2,1,0:T(8,128)(2,1)S(1)} %collective-permute-done.4), channel_id=4, replica_groups={{0,1},{2,3},{4,5},{6,7},{8,9},{10,11},{12,13},{14,15},{16,17},{18,19},{..., dimensions={0}, use_global_device_ids=true | all-gather | bytes 98304 | tf_op jit(solution)/shard_map/all_gather | solution.py:314
  48.4 7.2 %all_to_all.5 = bf16[4,2,64,128]{3,2,1,0:T(8,128)(2,1)S(1)} all-to-all(bf16[4,2,64,128]{3,2,1,0:T(8,128)(2,1)S(1)} %broadcast_in_dim.10), channel_id=1, replica_groups={{0,2,4,6},{1,3,5,7},{8,10,12,14},{9,11,13,15},{16,18,20,22},{17,19,21,2..., dimensions={0} | all-to-all | bytes 262144 | tf_op jit(solution)/shard_map/all_to_all | solution.py:321
  55.7 0.6 %fusion.5 = f32[2,1,64,128]{3,2,1,0:T(8,128)} fusion(f32[4,2,64,128]{3,2,1,0:T(8,128)S(1)} %convert_element_type.32), kind=kLoop, calls=%fused_computation.13 | loop fusion | flops 49152 | bytes 327680 | tf_op jit(solution)/shard_map/add | solution.py:322
  (4 shorter events, 0.1 us)
Async XLA Ops:
  1.9 30.0 %collective-permute-start = (bf16[2,3,2,32,128]{4,3,2,1,0:T(8,128)(2,1)S(1)}, bf16[2,3,2,32,128]{4,3,2,1,0:T(8,128)(2,1)S(1)}, u32[]{:S(2)}, u32[]{:S(2)}) collective-permute-start(bf16[2,3,2,32,128]{4,3,2,1,0:T(8,128)(2,1)S(1)} %get-tuple-element.12), channel_id=1, source_target_pairs={{24,48},{31,55},{48,24},{55,31},{72,96},{79,103},{96,72},{103,79},... | collective-permute-start | bytes 294920 | tf_op jit(solution)/shard_map/ppermute | solution.py:359
  2.5 29.4 %collective-permute-start.1 = (bf16[2,3,2,32,128]{4,3,2,1,0:T(8,128)(2,1)S(1)}, bf16[2,3,2,32,128]{4,3,2,1,0:T(8,128)(2,1)S(1)}, u32[]{:S(2)}, u32[]{:S(2)}) collective-permute-start(bf16[2,3,2,32,128]{4,3,2,1,0:T(8,128)(2,1)S(1)} %get-tuple-element.13), channel_id=1, source_target_pairs={{0,23},{1,2},{2,1},{3,4},{4,3},{5,6},{6,5},{7,8},{8,7},{9,10},{10,... | collective-permute-start | bytes 294920 | tf_op jit(solution)/shard_map/ppermute | solution.py:360
  7.1 24.8 %collective-permute-start.2 = (bf16[2,3,2,32,128]{4,3,2,1,0:T(8,128)(2,1)S(1)}, bf16[2,3,2,32,128]{4,3,2,1,0:T(8,128)(2,1)S(1)}, u32[]{:S(2)}, u32[]{:S(2)}) collective-permute-start(bf16[2,3,2,32,128]{4,3,2,1,0:T(8,128)(2,1)S(1)} %get-tuple-element.14), channel_id=1, source_target_pairs={{1,745},{2,746},{3,747},{4,748},{5,749},{6,750},{8,752},{9,753},{1... | collective-permute-start | bytes 294920 | tf_op jit(solution)/shard_map/ppermute | solution.py:361
  17.6 15.5 %collective-permute-start.3 = (bf16[2,3,2,32,128]{4,3,2,1,0:T(8,128)(2,1)S(1)}, bf16[2,3,2,32,128]{4,3,2,1,0:T(8,128)(2,1)S(1)}, u32[]{:S(2)}, u32[]{:S(2)}) collective-permute-start(bf16[2,3,2,32,128]{4,3,2,1,0:T(8,128)(2,1)S(1)} %get-tuple-element.15), channel_id=1, source_target_pairs={{0,24},{1,25},{2,26},{3,27},{4,28},{5,29},{6,30},{7,31},{8,32},{9,... | collective-permute-start | bytes 294920 | tf_op jit(solution)/shard_map/ppermute | solution.py:362
  19.5 12.4 %copy-start.1 = (bf16[2,2,3,3,1,1,128]{6,1,5,4,3,2,0:T(2,128)(2,1)S(1)}, bf16[2,2,3,3,1,1,128]{6,1,5,4,3,2,0:T(2,128)(2,1)}, u32[]{:S(2)}) copy-start(bf16[2,2,3,3,1,1,128]{6,1,5,4,3,2,0:T(2,128)(2,1)} %param.6) | copy-start | bytes 27652
  31.9 1.2 %copy-start = (bf16[2,3,64,1,1,128]{5,2,4,3,1,0:T(8,128)(2,1)S(1)}, bf16[2,3,64,1,1,128]{5,2,4,3,1,0:T(8,128)(2,1)}, u32[]{:S(2)}) copy-start(bf16[2,3,64,1,1,128]{5,2,4,3,1,0:T(8,128)(2,1)} %param.7) | copy-start | bytes 294916
  36.8 8.6 %collective-permute-start.4 = (bf16[2,64,128]{2,1,0:T(8,128)(2,1)S(1)}, bf16[2,64,128]{2,1,0:T(8,128)(2,1)S(1)}, u32[]{:S(2)}, u32[]{:S(2)}) collective-permute-start(bf16[2,64,128]{2,1,0:T(8,128)(2,1)S(1)} %fusion.7), channel_id=1, source_target_pairs={{0,16},{1,9},{2,18},{3,11},{4,20},{5,13},{6,22},{7,15},{8,0},{9,17... | collective-permute-start | bytes 98312 | tf_op jit(solution)/shard_map/ppermute | solution.py:311
